TPU v7x, 128 devices: a whole 4x4x4 slice. The times are simulated.
128 devices in a mesh: group: 4 (over z_lo, core), tp: 32 (over y, z_hi, x).
Axes of the slice: x: 4, y: 4, z: 4 (z_hi: 2, z_lo: 2; z = z_hi * 2 + z_lo), core: 2. Of those that a mesh axis runs over, the one named last changes fastest.
Arguments:
- hidden_states: bfloat16 [4, 768, 8192], P(None, ('group', 'tp')), may hold values from -400 to 400
- norm_gain: bfloat16 [8192], replicated, may hold values from 0.099609375 to 1.8984375
- lengths: int32 [768], P(('group', 'tp')), may hold values from 2 to 512, as said below
- rotated_key_cache: bfloat16 [768, 512, 1024], P(('group', 'tp')), may hold values from -80 to 80
- value_cache: bfloat16 [768, 512, 1024], P(('group', 'tp')), may hold values from -8 to 8
- qkv_weight: bfloat16 [8192, 10240], P(('group', 'tp')), may hold values from -0.0625 to 0.0625
- qkv_grad: bfloat16 [8192, 10240], P(('group', 'tp')), may hold values from -6 to 6
- qkv_first: bfloat16 [8192, 10240], P(('group', 'tp')), may hold values from -0.59765625 to 0.59765625
- qkv_second: bfloat16 [8192, 10240], P(('group', 'tp')), may hold values from 0.0049743652 to 0.19921875
- out_weight: bfloat16 [8192, 8192], P(('group', 'tp')), may hold values from -0.0625 to 0.0625
- out_grad: bfloat16 [8192, 8192], P(('group', 'tp')), may hold values from -6 to 6
- out_first: bfloat16 [8192, 8192], P(('group', 'tp')), may hold values from -0.59765625 to 0.59765625
- out_second: bfloat16 [8192, 8192], P(('group', 'tp')), may hold values from 0.0049743652 to 0.19921875
Outputs:
- layer_out: bfloat16 [4, 768, 8192], P(None, 'group', 'tp')
Inputs may be any that keep to these rules, and one draw needn't show every extreme that they name: `lengths`: in each aligned block of 6 rows one row has length 512.
All inputs are finite; a program needn't handle non-finite values.
Results may differ from a plain program's by a relative error of at most 0.011.
The roundings to bfloat16 on the way count: a program that leaves them out, or rounds other values in their place, can miss the bound.
Values may be sent and summed in bfloat16 or wider, within the bound.
No kernel may reach another device: no remote copies, remote signals or barrier semaphores. Data moves between devices by JAX's collectives and lax.ppermute only.
A program may use at most 192 MiB of HBM per device.

v0:
```python
import functools
import math

import jax
import jax.numpy as jnp
from jax import lax
from jax.experimental import pallas as pl
from jax.experimental.pallas import tpu as pltpu
from jax.sharding import PartitionSpec as P

D = 8192
HQ = 64
KEY_HEADS = 8
HEAD_SIZE = 128
CONTEXT_SLOTS = 512
DECODE_STEPS = 4
QUERY_WIDTH = 8192
KEY_WIDTH = 1024


learn_rate = 0.008
beta_one = 0.9
beta_two = 0.95
bias_one = 1.0 - beta_one * beta_one
bias_two = 1.0 - beta_two * beta_two
adam_eps = 1e-08
decay_rate = 0.1
rope_base = 500000.0
norm_eps = 1e-05


def adam_step(weight, gradient, moment_one, moment_two):
    grad_wide = gradient.astype(jnp.float32)
    first_new = beta_one * moment_one.astype(jnp.float32) + (1.0 - beta_one) * grad_wide
    second_new = (
        beta_two * moment_two.astype(jnp.float32) + (1.0 - beta_two) * grad_wide * grad_wide
    )
    weight_wide = weight.astype(jnp.float32)
    update = (
        first_new / bias_one / (jnp.sqrt(second_new / bias_two) + adam_eps)
        + decay_rate * weight_wide
    )
    return (weight_wide - learn_rate * update).astype(jnp.bfloat16)


PAIRS = 3
Z_SIZE = 4
PLANE = ("y", "x")


def shift_z(value, step):
    def position(z):
        return (z % 2) * 2 + (z // 2) % 2

    return lax.ppermute(
        value, ("zl", "zh"), [(position(z), position(z + step + Z_SIZE)) for z in range(Z_SIZE)]
    )


def swap_cores(value):
    return lax.ppermute(value, "c", [(0, 1), (1, 0)])


def norm_kernel(place_ref, hidden_ref, gain_ref, out_ref, scratch_ref):
    gain = gain_ref[...].astype(jnp.float32)
    rows = hidden_ref.shape[1]
    for step in range(DECODE_STEPS):
        wide = hidden_ref[step].astype(jnp.float32)
        inverse = lax.rsqrt(jnp.mean(wide * wide, axis=-1, keepdims=True) + norm_eps)
        normed = wide * inverse * gain
        for row in range(rows):
            at = row * DECODE_STEPS + step
            scratch_ref[at : at + 1, :] = normed[row : row + 1]
    for block in range(D // 256):
        start = pl.multiple_of(place_ref[block] * 256, 256)
        out_ref[:, pl.ds(start, 256)] = scratch_ref[
            :, block * 256 : (block + 1) * 256
        ].astype(jnp.bfloat16)


def norm_rows(hidden_states, norm_gain, places):
    rows = DECODE_STEPS * hidden_states.shape[1]
    vmem = pl.BlockSpec(memory_space=pltpu.VMEM)
    return pl.pallas_call(
        norm_kernel,
        out_shape=jax.ShapeDtypeStruct((rows, D), jnp.bfloat16),
        in_specs=[pl.BlockSpec(memory_space=pltpu.SMEM), vmem, vmem],
        out_specs=vmem,
        scratch_shapes=[pltpu.VMEM((rows, D), jnp.float32)],
        compiler_params=pltpu.CompilerParams(vmem_limit_bytes=16 * 1024 * 1024),
        name="norm_rows",
    )(places, hidden_states, norm_gain[None])


def rotary_tables(lengths):
    half_width = HEAD_SIZE // 2
    frequency = jnp.power(
        rope_base, -2.0 * jnp.arange(half_width, dtype=jnp.float32) / HEAD_SIZE
    )
    positions = lengths[:, None] + jnp.arange(DECODE_STEPS, dtype=jnp.int32)[None, :]
    angles = positions.astype(jnp.float32)[..., None] * frequency
    cosine, sine = jnp.cos(angles), jnp.sin(angles)
    shape = (PAIRS, 8, HEAD_SIZE)
    return (
        jnp.concatenate([cosine, cosine], axis=-1).reshape(shape),
        jnp.concatenate([-sine, sine], axis=-1).reshape(shape),
    )


def attention_kernel(lengths_ref, field_ref, cos_ref, sin_ref, key_ref, value_ref, out_ref):
    pair = pl.program_id(0)
    cosine, sine = cos_ref[0], sin_ref[0]
    scale = 1.0 / math.sqrt(HEAD_SIZE)
    row = lax.broadcasted_iota(jnp.int32, (64, 1), 0)
    second_row = ((row >> 2) & 1) == 1
    step = row & 3
    length = jnp.where(second_row, lengths_ref[2 * pair + 1], lengths_ref[2 * pair])
    live = lax.broadcasted_iota(jnp.int32, (64, CONTEXT_SLOTS), 1) < length
    fresh_column = lax.broadcasted_iota(jnp.int32, (64, 8), 1)
    fresh_live = (((fresh_column >> 2) & 1) == ((row >> 2) & 1)) & ((fresh_column & 3) <= step)

    def field(block, start):
        return field_ref[block, 0, :, start : start + 128].astype(jnp.float32)

    def rotate(vector):
        return vector * cosine + pltpu.roll(vector, 64, 1) * sine

    def times_transposed(left, right):
        return lax.dot_general(
            left, right, (((1,), (1,)), ((), ())), preferred_element_type=jnp.float32
        )

    for kv in range(KEY_HEADS):
        columns = slice(kv * HEAD_SIZE, (kv + 1) * HEAD_SIZE)
        query = jnp.concatenate(
            [rotate(field(2 * kv + h // 4, (h % 4) * 128)) for h in range(8)], axis=0
        ).astype(jnp.bfloat16)
        fresh_key = rotate(field(kv, 512)).astype(jnp.bfloat16)
        fresh_value = field(8 + kv, 512).astype(jnp.bfloat16)
        scores = jnp.where(
            second_row,
            times_transposed(query, key_ref[1, :, columns]),
            times_transposed(query, key_ref[0, :, columns]),
        ) * scale
        fresh_scores = times_transposed(query, fresh_key) * scale
        scores = jnp.where(live, scores, -jnp.inf)
        fresh_scores = jnp.where(fresh_live, fresh_scores, -jnp.inf)
        highest = jnp.maximum(
            jnp.max(scores, axis=-1, keepdims=True), jnp.max(fresh_scores, axis=-1, keepdims=True)
        )
        weight = jnp.exp(scores - highest)
        fresh_weight = jnp.exp(fresh_scores - highest)
        inverse = 1.0 / (
            jnp.sum(weight, axis=-1, keepdims=True) + jnp.sum(fresh_weight, axis=-1, keepdims=True)
        )
        prob = weight * inverse
        fresh_prob = (fresh_weight * inverse).astype(jnp.bfloat16)
        attended = (
            jnp.dot(
                jnp.where(second_row, 0.0, prob).astype(jnp.bfloat16),
                value_ref[0, :, columns],
                preferred_element_type=jnp.float32,
            )
            + jnp.dot(
                jnp.where(second_row, prob, 0.0).astype(jnp.bfloat16),
                value_ref[1, :, columns],
                preferred_element_type=jnp.float32,
            )
            + jnp.dot(fresh_prob, fresh_value, preferred_element_type=jnp.float32)
        )
        for h in range(0, 8, 2):
            natural = 4 * kv + h // 2
            y = (natural >> 1) & 3
            start = ((natural >> 3) * 2 + (natural & 1)) * 256
            block = jnp.concatenate(
                [attended[8 * h : 8 * h + 8], attended[8 * h + 8 : 8 * h + 16]], axis=1
            ).astype(jnp.bfloat16)
            for x in range(4):
                out_ref[4 * y + x, 0, :, start : start + 256] = block


def attention(fields, cosine, sine, keys, values, lengths):
    table = pl.BlockSpec((1, 8, HEAD_SIZE), lambda i, *_: (i, 0, 0))
    cache = pl.BlockSpec((2, CONTEXT_SLOTS, KEY_WIDTH), lambda i, *_: (i, 0, 0))
    return pl.pallas_call(
        attention_kernel,
        out_shape=jax.ShapeDtypeStruct((16, PAIRS, 8, 2048), jnp.bfloat16),
        grid_spec=pltpu.PrefetchScalarGridSpec(
            num_scalar_prefetch=1,
            grid=(PAIRS,),
            in_specs=[
                pl.BlockSpec((16, 1, 8, 640), lambda i, *_: (0, i, 0, 0)),
                table,
                table,
                cache,
                cache,
            ],
            out_specs=pl.BlockSpec((16, 1, 8, 2048), lambda i, *_: (0, i, 0, 0)),
        ),
        compiler_params=pltpu.CompilerParams(vmem_limit_bytes=40 * 1024 * 1024),
        cost_estimate=pl.CostEstimate(
            flops=PAIRS * 8 * 8 * 64 * 512 * 128,
            bytes_accessed=PAIRS * 4 * 1024 * 1024,
            transcendentals=PAIRS * 8 * 64 * 512,
        ),
        name="attention",
    )(lengths, fields, cosine, sine, keys, values)


def out_kernel(rows_ref, weight_ref, out_ref):
    out_ref[0] = jnp.dot(
        rows_ref[...], weight_ref[...], preferred_element_type=jnp.float32
    ).astype(jnp.bfloat16)


def out_partial(rows, weight):
    count, depth = rows.shape
    blocks = weight.shape[1] // 256
    return pl.pallas_call(
        out_kernel,
        out_shape=jax.ShapeDtypeStruct((blocks, count, 256), jnp.bfloat16),
        grid=(blocks,),
        in_specs=[
            pl.BlockSpec((count, depth), lambda i: (0, 0)),
            pl.BlockSpec((depth, 256), lambda i: (0, i)),
        ],
        out_specs=pl.BlockSpec((1, count, 256), lambda i: (i, 0, 0)),
        compiler_params=pltpu.CompilerParams(vmem_limit_bytes=24 * 1024 * 1024),
        cost_estimate=pl.CostEstimate(
            flops=2 * count * depth * blocks * 256,
            bytes_accessed=2 * depth * blocks * 256,
            transcendentals=0,
        ),
        name="out_partial",
    )(rows, weight)


def block_places():
    z_index = lax.axis_index("zh") * 2 + lax.axis_index("zl")
    natural = jnp.arange(32, dtype=jnp.int32)
    zl, c, y, zh = natural >> 4, (natural >> 3) & 1, (natural >> 1) & 3, natural & 1
    plane = (zh * 2 + zl - z_index + 4) & 3
    core = (c - lax.axis_index("c") + 2) & 1
    return (plane * 2 + core) * 4 + y


def body(
    hidden_states,
    norm_gain,
    lengths,
    rotated_key_cache,
    value_cache,
    qkv_weight,
    qkv_grad,
    qkv_first,
    qkv_second,
    out_weight,
    out_grad,
    out_first,
    out_second,
):
    depth = qkv_weight.shape[0]

    normed = norm_rows(hidden_states, norm_gain, block_places())
    normed_rows = lax.all_gather(normed, PLANE, axis=0, tiled=True)

    qkv_updated = adam_step(qkv_weight, qkv_grad, qkv_first, qkv_second)
    qkv_piece = jnp.concatenate(
        [
            qkv_updated[:, :QUERY_WIDTH].reshape(depth, 16, 512),
            qkv_updated[:, QUERY_WIDTH:].reshape(depth, 16, 128),
        ],
        axis=2,
    ).transpose(1, 0, 2)
    qkv_own = lax.all_to_all(qkv_piece, PLANE, split_axis=0, concat_axis=0, tiled=True)
    qkv_own = qkv_own.reshape(16 * depth, 640)
    half = qkv_own.shape[0] // 2
    below = shift_z(qkv_own, 1)
    above = shift_z(qkv_own, -1)

    out_updated = adam_step(out_weight, out_grad, out_first, out_second)
    out_piece = out_updated.reshape(depth, 8, 4, 256).transpose(2, 0, 1, 3).reshape(4, depth, 2048)
    out_piece, qkv_own = lax.optimization_barrier((out_piece, qkv_own))
    out_own = lax.all_to_all(out_piece, "x", split_axis=0, concat_axis=0, tiled=True)
    out_own = out_own.reshape(4 * depth, 2048)

    far = jnp.concatenate([shift_z(below[:half], 1), shift_z(above[half:], -1)], axis=0)
    cosine, sine = rotary_tables(lengths)
    far, out_own, cosine, sine = lax.optimization_barrier((far, out_own, cosine, sine))
    out_owned = lax.all_gather(out_own, ("zl", "c", "zh"), axis=0, tiled=True)

    projected = None
    for plane, weight in ((0, qkv_own), (1, above), (3, below), (2, far)):
        for core, part in enumerate((weight, swap_cores(weight))):
            start = (2 * plane + core) * 1024
            term = jnp.dot(
                normed_rows[:, start : start + 1024], part, preferred_element_type=jnp.float32
            )
            projected = term if projected is None else projected + term
    projected = projected.astype(jnp.bfloat16).reshape(16, -1, 640)
    fields = lax.all_to_all(projected, PLANE, split_axis=0, concat_axis=0, tiled=True)

    attended = attention(
        fields.reshape(16, PAIRS, 8, 640), cosine, sine, rotated_key_cache, value_cache, lengths
    )
    attended = lax.all_to_all(attended, PLANE, split_axis=0, concat_axis=0, tiled=True)
    partial = out_partial(attended.reshape(-1, 2048), out_owned)
    partial = lax.all_to_all(partial, ("y", "zh"), split_axis=0, concat_axis=0, tiled=True)
    total = jnp.sum(partial.reshape(4, 2, -1, 256).astype(jnp.float32), axis=0)
    total = total.astype(jnp.bfloat16).reshape(2, 4, 4, -1, DECODE_STEPS, 256)
    return total.transpose(4, 1, 0, 2, 3, 5).reshape(DECODE_STEPS, -1, 256)


def solution(mesh):
    every = ("zl", "c", "y", "zh", "x")
    fine = jax.sharding.Mesh(mesh.devices.reshape(2, 2, 4, 2, 4), every)
    return jax.shard_map(
        body,
        mesh=fine,
        in_specs=(
            P(None, every, None),
            P(),
            P(every),
            P(every, None, None),
            P(every, None, None),
        )
        + (P(every, None),) * 8,
        out_specs=P(None, ("zl", "c"), ("y", "zh", "x")),
        check_vma=False,
    )
```

profile of v0, /device:TPU:0, one launch (start us, length us, event | category | flops | bytes accessed | tf_op | source)
XLA Modules:
  0.0 317.0 jit_solution(13023686328242517126)
XLA Ops:
  6.5 1.3 copy.25.hidden_ref
  7.9 0.7 broadcast_in_dim.2.gain_ref
  8.6 1.9 norm_rows.1
  10.6 4.4 %fusion.2 = bf16[64,10240]{1,0:T(8,128)(2,1)S(1)} fusion(bf16[64,10240]{1,0:T(8,128)(2,1)S(1)} %copy-done.5, bf16[64,10240]{1,0:T(8,128)(2,1)} %param.19, bf16[64,10240]{1,0:T(8,128)(2,1)} %param.21, bf16[64,10240]{1,0:T(8,128)(2,1)} %param.20), kind=kLoop, calls=%fused_computation.10 | loop fusion | flops 13107200 | bytes 6553600 | tf_op jit(solution)/shard_map/convert_element_type | solution.py:43
  15.1 0.4 copy.31
  15.5 0.1 maximum_bitcast_fusion
  15.7 0.3 copy.27
  16.0 33.5 %all_to_all.25 = bf16[16,64,640]{2,1,0:T(8,128)(2,1)S(1)} all-to-all(bf16[16,64,640]{2,1,0:T(8,128)(2,1)S(1)} %copy.27), channel_id=1, replica_groups=mesh['zl'=2,'c'=2,'y'=4,'zh'=2,'x'=4] {'y','x'}, dimensions={0} | all-to-all | bytes 2621440 | tf_op jit(solution)/shard_map/all_to_all | solution.py:275
  49.5 3.5 %collective-permute-start.1 = (bf16[1024,640]{1,0:T(8,128)(2,1)S(1)}, bf16[1024,640]{1,0:T(8,128)(2,1)}, u32[]{:S(2)}, u32[]{:S(2)}) collective-permute-start(bf16[1024,640]{1,0:T(8,128)(2,1)S(1)} %bitcast.39), channel_id=1, source_target_pairs={{0,68},{64,0},{4,64},{68,4},{1,69},{65,1},{5,65},{69,5},{2,70},{66... | collective-permute-start | bytes 3932168 | tf_op jit(solution)/shard_map/ppermute | solution.py:55
  53.0 1.9 fusion.12
  54.9 0.8 reshape.78
  55.7 0.1 copy.26
  55.8 1.3 reshape.79
  57.3 0.1 add.117
  57.5 3.5 %all-to-all-start.1 = ((bf16[4,64,2048]{2,1,0:T(8,128)(2,1)}), bf16[4,64,2048]{2,1,0:T(8,128)(2,1)S(1)}, u32[]{:S(2)}, u32[]{:S(2)}) async-start(bf16[4,64,2048]{2,1,0:T(8,128)(2,1)} %reshape.79), calls=%async_computation.1 | async-start | bytes 2097152 | tf_op jit(solution)/shard_map/all_to_all | solution.py:284
  61.1 22.9 %collective-permute-done.3 = bf16[1024,640]{1,0:T(8,128)(2,1)} collective-permute-done((bf16[1024,640]{1,0:T(8,128)(2,1)S(1)}, bf16[1024,640]{1,0:T(8,128)(2,1)}, u32[]{:S(2)}, u32[]{:S(2)}) %collective-permute-start.3) | collective-permute-done | bytes 1310752 | tf_op jit(solution)/shard_map/ppermute | solution.py:55
  84.0 1.2 slice.57
  85.3 1.1 slice.58
  86.4 3.3 %collective-permute-start.6 = (bf16[512,640]{1,0:T(8,128)(2,1)S(1)}, bf16[512,640]{1,0:T(8,128)(2,1)S(1)}, u32[]{:S(2)}, u32[]{:S(2)}) collective-permute-start(bf16[512,640]{1,0:T(8,128)(2,1)S(1)} %slice.58), channel_id=1, source_target_pairs={{0,68},{64,0},{4,64},{68,4},{1,69},{65,1},{5,65},{69,5},{2,70},{66... | collective-permute-start | bytes 1966088 | tf_op jit(solution)/shard_map/ppermute | solution.py:55
  89.7 0.1 fusion.34
  90.0 11.3 %collective-permute-done.5 = bf16[512,640]{1,0:T(8,128)(2,1)S(1)} collective-permute-done((bf16[512,640]{1,0:T(8,128)(2,1)S(1)}, bf16[512,640]{1,0:T(8,128)(2,1)S(1)}, u32[]{:S(2)}, u32[]{:S(2)}) %collective-permute-start.5) | collective-permute-done | bytes 655392 | tf_op jit(solution)/shard_map/ppermute | solution.py:55
  101.2 0.5 collective-permute-done.6
  101.7 1.2 pad_maximum_fusion
  102.9 1.0 copy-done.2
  103.9 0.1 collective-permute-start
  104.0 0.5 collective-permute-start.2
  104.5 0.1 collective-permute-start.4
  104.6 0.4 collective-permute-start.7
  105.1 2.1 fusion.32
  107.1 2.3 fusion.27
  109.5 0.8 convolution_add_fusion.4
  110.3 0.5 copy-done.4
  110.8 0.8 fusion.24
  111.6 2.1 convolution_add_fusion.3
  113.7 2.2 fusion.21
  116.0 2.3 fusion.20
  118.2 2.1 fusion.22
  120.3 14.5 %all_to_all.26 = bf16[16,24,640]{2,1,0:T(8,128)(2,1)S(1)} all-to-all(bf16[16,24,640]{2,1,0:T(8,128)(2,1)S(1)} %bitcast.44), channel_id=1, replica_groups=mesh['zl'=2,'c'=2,'y'=4,'zh'=2,'x'=4] {'y','x'}, dimensions={0} | all-to-all | bytes 983040 | tf_op jit(solution)/shard_map/all_to_all | solution.py:301
  134.9 13.3 %attention.1 = bf16[16,3,8,2048]{3,2,1,0:T(8,128)(2,1)S(1)} custom-call(s32[6]{0:T(128)S(1)} %copy-done, bf16[16,3,8,640]{3,2,1,0:T(8,128)(2,1)S(1)} %bitcast.30, f32[3,8,128]{2,1,0:T(8,128)S(1)} %get-tuple-element.14.cos_ref, f32[3,8,128]{2,1,0:T(8,128)S(1)} %get-tuple-element.15.sin_ref, bf16[6,512,1024]{2,1,0:T(8,128)(2,1)S(1)} %bitcast.29, ...), custom_call_target="tpu_custom_call" | custom-call | flops 805306368 | bytes 12582912 | tf_op jit(solution)/shard_map/attention/pallas_call | solution.py:185
  148.2 25.3 %all_to_all.27 = bf16[16,3,8,2048]{3,2,1,0:T(8,128)(2,1)S(1)} all-to-all(bf16[16,3,8,2048]{3,2,1,0:T(8,128)(2,1)S(1)} %attention.1), channel_id=1, replica_groups=mesh['zl'=2,'c'=2,'y'=4,'zh'=2,'x'=4] {'y','x'}, dimensions={0} | all-to-all | bytes 3145728 | tf_op jit(solution)/shard_map/all_to_all | solution.py:306
  173.5 98.7 %all-gather.5.cloned.1.call-done.weight_ref = bf16[2048,2048]{1,0:T(8,128)(2,1)} async-done(((bf16[256,2048]{1,0:T(8,128)(2,1)}), bf16[2048,2048]{1,0:T(8,128)(2,1)}) %all-gather.5.cloned.1.call-update) | async-done | bytes 8388624 | tf_op jit(solution)/shard_map/all_gather | solution.py:290
  272.1 3.4 %copy-done.1 = bf16[2048,2048]{1,0:T(8,128)(2,1)S(1)} copy-done((bf16[2048,2048]{1,0:T(8,128)(2,1)S(1)}, bf16[2048,2048]{1,0:T(8,128)(2,1)}, u32[]{:S(2)}) %copy-start.1) | copy-done | bytes 8388632
  275.5 5.9 %out_partial.1 = bf16[8,384,256]{2,1,0:T(8,128)(2,1)S(1)} custom-call(bf16[384,2048]{1,0:T(8,128)(2,1)S(1)} %bitcast.31, bf16[2048,2048]{1,0:T(8,128)(2,1)S(1)} %copy-done.1), custom_call_target="tpu_custom_call" | custom-call | flops 3221225472 | bytes 8388608 | tf_op jit(solution)/shard_map/out_partial/pallas_call | solution.py:219
  281.4 26.9 %all_to_all.28 = bf16[8,384,256]{2,1,0:T(8,128)(2,1)S(1)} all-to-all(bf16[8,384,256]{2,1,0:T(8,128)(2,1)S(1)} %out_partial.1), channel_id=1, replica_groups=mesh['zl'=2,'c'=2,'y'=4,'zh'=2,'x'=4] {'y','zh'}, dimensions={0} | all-to-all | bytes 3145728 | tf_op jit(solution)/shard_map/all_to_all | solution.py:308
  308.3 0.4 reduce_sum.12
  308.8 0.4 copy.28
  309.2 0.2 copy.29
  309.3 0.8 copy.30
  (46 shorter events, 0.7 us)
Async XLA Ops:
  6.5 4.0 %copy-start.5 = (bf16[64,10240]{1,0:T(8,128)(2,1)S(1)}, bf16[64,10240]{1,0:T(8,128)(2,1)}, u32[]{:S(2)}) copy-start(bf16[64,10240]{1,0:T(8,128)(2,1)} %param.18) | copy-start | bytes 3932164
  6.5 98.5 %all-gather.3.cloned.1.call-start = ((), (), s32[]{:S(2)}) async-start(), calls=%async_computation.5 | async-start | bytes 6684672 | tf_op jit(solution)/shard_map/all_gather | solution.py:265
  15.7 37.3 %copy-start.6 = (bf16[64,8192]{1,0:T(8,128)(2,1)S(1)}, bf16[64,8192]{1,0:T(8,128)(2,1)}, u32[]{:S(2)}) copy-start(bf16[64,8192]{1,0:T(8,128)(2,1)} %param.22) | copy-start | bytes 3145732
  15.7 37.3 %copy-start.7 = (bf16[64,8192]{1,0:T(8,128)(2,1)S(1)}, bf16[64,8192]{1,0:T(8,128)(2,1)}, u32[]{:S(2)}) copy-start(bf16[64,8192]{1,0:T(8,128)(2,1)} %param.23) | copy-start | bytes 3145732
  15.7 37.3 %copy-start.8 = (bf16[64,8192]{1,0:T(8,128)(2,1)S(1)}, bf16[64,8192]{1,0:T(8,128)(2,1)}, u32[]{:S(2)}) copy-start(bf16[64,8192]{1,0:T(8,128)(2,1)} %param.25) | copy-start | bytes 3145732
  15.7 37.3 %copy-start.9 = (bf16[64,8192]{1,0:T(8,128)(2,1)S(1)}, bf16[64,8192]{1,0:T(8,128)(2,1)}, u32[]{:S(2)}) copy-start(bf16[64,8192]{1,0:T(8,128)(2,1)} %param.24) | copy-start | bytes 3145732
  49.5 35.8 %collective-permute-start.1 = (bf16[1024,640]{1,0:T(8,128)(2,1)S(1)}, bf16[1024,640]{1,0:T(8,128)(2,1)}, u32[]{:S(2)}, u32[]{:S(2)}) collective-permute-start(bf16[1024,640]{1,0:T(8,128)(2,1)S(1)} %bitcast.39), channel_id=1, source_target_pairs={{0,68},{64,0},{4,64},{68,4},{1,69},{65,1},{5,65},{69,5},{2,70},{66... | collective-permute-start | bytes 3932168 | tf_op jit(solution)/shard_map/ppermute | solution.py:55
  53.0 31.1 %collective-permute-start.3 = (bf16[1024,640]{1,0:T(8,128)(2,1)S(1)}, bf16[1024,640]{1,0:T(8,128)(2,1)}, u32[]{:S(2)}, u32[]{:S(2)}) collective-permute-start(bf16[1024,640]{1,0:T(8,128)(2,1)S(1)} %bitcast.40), channel_id=1, source_target_pairs={{0,64},{64,4},{4,68},{68,0},{1,65},{65,5},{5,69},{69,1},{2,66},{66... | collective-permute-start | bytes 3932168 | tf_op jit(solution)/shard_map/ppermute | solution.py:55
  55.7 1.5 copy-start
  57.5 45.4 %all-to-all-start.1 = ((bf16[4,64,2048]{2,1,0:T(8,128)(2,1)}), bf16[4,64,2048]{2,1,0:T(8,128)(2,1)S(1)}, u32[]{:S(2)}, u32[]{:S(2)}) async-start(bf16[4,64,2048]{2,1,0:T(8,128)(2,1)} %reshape.79), calls=%async_computation.1 | async-start | bytes 2097152 | tf_op jit(solution)/shard_map/all_to_all | solution.py:284
  61.0 211.1 %all-gather.5.cloned.1.call-start = ((), (), s32[]{:S(2)}) async-start(), calls=%async_computation.6 | async-start | bytes 9437184 | tf_op jit(solution)/shard_map/all_gather | solution.py:290
  85.2 16.0 %collective-permute-start.5 = (bf16[512,640]{1,0:T(8,128)(2,1)S(1)}, bf16[512,640]{1,0:T(8,128)(2,1)S(1)}, u32[]{:S(2)}, u32[]{:S(2)}) collective-permute-start(bf16[512,640]{1,0:T(8,128)(2,1)S(1)} %slice.57), channel_id=1, source_target_pairs={{0,64},{64,4},{4,68},{68,0},{1,65},{65,5},{5,69},{69,1},{2,66},{66... | collective-permute-start | bytes 1966088 | tf_op jit(solution)/shard_map/ppermute | solution.py:55
  86.4 15.3 %collective-permute-start.6 = (bf16[512,640]{1,0:T(8,128)(2,1)S(1)}, bf16[512,640]{1,0:T(8,128)(2,1)S(1)}, u32[]{:S(2)}, u32[]{:S(2)}) collective-permute-start(bf16[512,640]{1,0:T(8,128)(2,1)S(1)} %slice.58), channel_id=1, source_target_pairs={{0,68},{64,0},{4,64},{68,4},{1,69},{65,1},{5,65},{69,5},{2,70},{66... | collective-permute-start | bytes 1966088 | tf_op jit(solution)/shard_map/ppermute | solution.py:55
  102.9 1.0 copy-start.2
  103.9 5.5 %collective-permute-start = (bf16[1024,640]{1,0:T(8,128)(2,1)S(1)}, bf16[1024,640]{1,0:T(8,128)(2,1)S(1)}, u32[]{:S(2)}, u32[]{:S(2)}) collective-permute-start(bf16[1024,640]{1,0:T(8,128)(2,1)S(1)} %bitcast.41), channel_id=1, source_target_pairs={{0,32},{32,0},{1,33},{33,1},{2,34},{34,2},{3,35},{35,3},{4,36},{36... | collective-permute-start | bytes 3932168 | tf_op jit(solution)/shard_map/ppermute | solution.py:61
  104.0 9.6 %collective-permute-start.2 = (bf16[1024,640]{1,0:T(8,128)(2,1)}, bf16[1024,640]{1,0:T(8,128)(2,1)}, u32[]{:S(2)}, u32[]{:S(2)}) collective-permute-start(bf16[1024,640]{1,0:T(8,128)(2,1)} %collective-permute-done.1), channel_id=1, source_target_pairs={{0,32},{32,0},{1,33},{33,1},{2,34},{34,2},{3,35},{35,3},{4,36},{36... | collective-permute-start | bytes 3932168 | tf_op jit(solution)/shard_map/ppermute | solution.py:61
  104.5 11.4 %collective-permute-start.4 = (bf16[1024,640]{1,0:T(8,128)(2,1)}, bf16[1024,640]{1,0:T(8,128)(2,1)}, u32[]{:S(2)}, u32[]{:S(2)}) collective-permute-start(bf16[1024,640]{1,0:T(8,128)(2,1)} %collective-permute-done.3), channel_id=1, source_target_pairs={{0,32},{32,0},{1,33},{33,1},{2,34},{34,2},{3,35},{35,3},{4,36},{36... | collective-permute-start | bytes 3932168 | tf_op jit(solution)/shard_map/ppermute | solution.py:61
  104.6 13.6 %collective-permute-start.7 = (bf16[1024,640]{1,0:T(8,128)(2,1)}, bf16[1024,640]{1,0:T(8,128)(2,1)}, u32[]{:S(2)}, u32[]{:S(2)}) collective-permute-start(bf16[1024,640]{1,0:T(8,128)(2,1)} %pad_maximum_fusion), channel_id=1, source_target_pairs={{0,32},{32,0},{1,33},{33,1},{2,34},{34,2},{3,35},{35,3},{4,36},{36... | collective-permute-start | bytes 3932168 | tf_op jit(solution)/shard_map/ppermute | solution.py:61
  105.1 4.4 %copy-start.3 = (bf16[384,8192]{1,0:T(8,128)(2,1)S(1)}, bf16[384,8192]{1,0:T(8,128)(2,1)}, u32[]{:S(2)}) copy-start(bf16[384,8192]{1,0:T(8,128)(2,1)} %all-gather.3.cloned.1.call-done) | copy-start | bytes 18874372
  109.5 1.3 copy-start.4
  113.7 21.2 %slice-start = ((s8[6291456]{0:T(1024)(128)(4,1)}), s8[4194304]{0:T(1024)(128)(4,1)S(1)}, s32[]{:S(2)}) async-start(s8[6291456]{0:T(1024)(128)(4,1)} %bitcast.28), calls=%async_computation.7 | async-start | bytes 8388608
  115.9 18.9 %slice-start.1 = ((s8[6291456]{0:T(1024)(128)(4,1)}), s8[2097152]{0:T(1024)(128)(4,1)S(1)}, s32[]{:S(2)}) async-start(s8[6291456]{0:T(1024)(128)(4,1)} %bitcast.28), calls=%async_computation.8 | async-start | bytes 4194304
  272.1 3.4 %copy-start.1 = (bf16[2048,2048]{1,0:T(8,128)(2,1)S(1)}, bf16[2048,2048]{1,0:T(8,128)(2,1)}, u32[]{:S(2)}) copy-start(bf16[2048,2048]{1,0:T(8,128)(2,1)} %all-gather.5.cloned.1.call-done.weight_ref) | copy-start | bytes 25165828
Sparse Core Ops, SparseCore 0:
  10.7 85.2 all-gather.2
  104.1 168.0 all-gather.4
where the time goes:
time: 320 us; the launch traced here: 317 us
  waiting for transfers between devices  133 us (42%)
  blocking collectives  100 us (31%)
  Pallas kernels  21.1 us (7%)
  matrix products  14.7 us (5%)
  local copies, waits for them, and re-layouts  14 us (4%)
  between operations  13.7 us (4%)
  starting transfers between devices  11.5 us (4%)
  other arithmetic  8.3 us (3%)
    all_gather x1, waiting for transfers between devices, body(): out_owned = lax.all_gather(out_own, ('zl', 'c', 'zh'), axis=0, tiled=True)  98.7 us
    ppermute x4, waiting for transfers between devices, shift_z(): lax.ppermute(value, ('zl', 'zh'), [(position(z), position(z + step + Z_SI...  34.7 us
    all_to_all x1, blocking collectives, body(): lax.all_to_all(qkv_piece, PLANE, split_axis=0, concat_axis=0, tiled=True)  33.5 us
    all_to_all x1, blocking collectives, body(): lax.all_to_all(partial, ('y', 'zh'), split_axis=0, concat_axis=0, tiled=T...  26.9 us
    all_to_all x1, blocking collectives, body(): lax.all_to_all(attended, PLANE, split_axis=0, concat_axis=0, tiled=True)  25.3 us
    dot_general x8, matrix products, body(): jnp.dot(normed_rows[:, start:start + 1024], part, preferred_element_type=...  14.7 us
    all_to_all x1, blocking collectives, body(): lax.all_to_all(projected, PLANE, split_axis=0, concat_axis=0, tiled=True)  14.5 us
    pallas_call x1, Pallas kernels, attention(): pl.pallas_call(attention_kernel, out_shape=jax.ShapeDtypeStruct((16, PAIR...  13.3 us
  transfers between devices with their start and end apart: 11, of which 4 were waited for; matrix products, arithmetic and copies ran while one was open for 9% of the time, Pallas kernels for 4%

commit v1 on v0

v1 whole, which is shorter than its diff:
```python
import functools
import math

import jax
import jax.numpy as jnp
from jax import lax
from jax.experimental import pallas as pl
from jax.experimental.pallas import tpu as pltpu
from jax.sharding import PartitionSpec as P

D = 8192
HQ = 64
KEY_HEADS = 8
HEAD_SIZE = 128
CONTEXT_SLOTS = 512
DECODE_STEPS = 4
QUERY_WIDTH = 8192
KEY_WIDTH = 1024


learn_rate = 0.008
beta_one = 0.9
beta_two = 0.95
bias_one = 1.0 - beta_one * beta_one
bias_two = 1.0 - beta_two * beta_two
adam_eps = 1e-08
decay_rate = 0.1
rope_base = 500000.0
norm_eps = 1e-05


def adam_step(weight, gradient, moment_one, moment_two):
    grad_wide = gradient.astype(jnp.float32)
    first_new = beta_one * moment_one.astype(jnp.float32) + (1.0 - beta_one) * grad_wide
    second_new = (
        beta_two * moment_two.astype(jnp.float32) + (1.0 - beta_two) * grad_wide * grad_wide
    )
    weight_wide = weight.astype(jnp.float32)
    update = (
        first_new / bias_one / (jnp.sqrt(second_new / bias_two) + adam_eps)
        + decay_rate * weight_wide
    )
    return (weight_wide - learn_rate * update).astype(jnp.bfloat16)


PAIRS = 3
Z_SIZE = 4
PLANE = ("y", "x")
VMEM_LIMIT = 56 * 1024 * 1024


def shift_z(value, step):
    def position(z):
        return (z % 2) * 2 + (z // 2) % 2

    return lax.ppermute(
        value, ("zl", "zh"), [(position(z), position(z + step + Z_SIZE)) for z in range(Z_SIZE)]
    )


def swap_cores(value):
    return lax.ppermute(value, "c", [(0, 1), (1, 0)])


def norm_kernel(place_ref, hidden_ref, gain_ref, out_ref, scratch_ref):
    gain = gain_ref[...].astype(jnp.float32)
    rows = hidden_ref.shape[1]
    for step in range(DECODE_STEPS):
        wide = hidden_ref[step].astype(jnp.float32)
        inverse = lax.rsqrt(jnp.mean(wide * wide, axis=-1, keepdims=True) + norm_eps)
        normed = wide * inverse * gain
        for row in range(rows):
            at = row * DECODE_STEPS + step
            scratch_ref[at : at + 1, :] = normed[row : row + 1]
    for natural in range(D // 256):
        start = pl.multiple_of(place_ref[natural] * 256, 256)
        block = scratch_ref[:, natural * 256 : (natural + 1) * 256].astype(jnp.bfloat16)
        for x in range(4):
            out_ref[4 * ((natural >> 1) & 3) + x, :, pl.ds(start, 256)] = block


def norm_rows(hidden_states, norm_gain, places):
    rows = DECODE_STEPS * hidden_states.shape[1]
    vmem = pl.BlockSpec(memory_space=pltpu.VMEM)
    return pl.pallas_call(
        norm_kernel,
        out_shape=jax.ShapeDtypeStruct((16, rows, D // 4), jnp.bfloat16),
        in_specs=[pl.BlockSpec(memory_space=pltpu.SMEM), vmem, vmem],
        out_specs=vmem,
        scratch_shapes=[pltpu.VMEM((rows, D), jnp.float32)],
        compiler_params=pltpu.CompilerParams(vmem_limit_bytes=16 * 1024 * 1024),
        name="norm_rows",
    )(places, hidden_states, norm_gain[None])


def rotary_tables(lengths):
    half_width = HEAD_SIZE // 2
    frequency = jnp.power(
        rope_base, -2.0 * jnp.arange(half_width, dtype=jnp.float32) / HEAD_SIZE
    )
    positions = lengths[:, None] + jnp.arange(DECODE_STEPS, dtype=jnp.int32)[None, :]
    angles = positions.astype(jnp.float32)[..., None] * frequency
    cosine, sine = jnp.cos(angles), jnp.sin(angles)
    shape = (PAIRS, 8, HEAD_SIZE)
    return (
        jnp.concatenate([cosine, cosine], axis=-1).reshape(shape),
        jnp.concatenate([-sine, sine], axis=-1).reshape(shape),
    )


def attention_kernel(
    lengths_ref, place_ref, field_ref, cos_ref, sin_ref, key_ref, value_ref, out_ref
):
    pair = pl.program_id(0)
    cosine, sine = cos_ref[0], sin_ref[0]
    scale = 1.0 / math.sqrt(HEAD_SIZE)
    line = lax.broadcasted_iota(jnp.int32, (128, 1), 0)
    second_row = ((line >> 2) & 1) == 1
    step = line & 3
    length = jnp.where(second_row, lengths_ref[2 * pair + 1], lengths_ref[2 * pair])
    live = lax.broadcasted_iota(jnp.int32, (128, CONTEXT_SLOTS), 1) < length
    fresh_column = lax.broadcasted_iota(jnp.int32, (128, 8), 1)
    fresh_live = (((fresh_column >> 2) & 1) == ((line >> 2) & 1)) & ((fresh_column & 3) <= step)

    def field(x, start):
        total = None
        for y in range(4):
            term = field_ref[4 * y + x, 0, :, start : start + 128].astype(jnp.float32)
            total = term if total is None else total + term
        return total.astype(jnp.bfloat16).astype(jnp.float32)

    def rotate(vector):
        return vector * cosine + pltpu.roll(vector, 64, 1) * sine

    def times_transposed(left, right):
        return lax.dot_general(
            left, right, (((1,), (1,)), ((), ())), preferred_element_type=jnp.float32
        )

    for x in range(KEY_HEADS // 2):
        cached, fresh, fresh_values = [], [], []
        for side in range(2):
            kv = 2 * x + side
            columns = slice(kv * HEAD_SIZE, (kv + 1) * HEAD_SIZE)
            query = jnp.concatenate(
                [rotate(field(x, (8 * side + h) * 128)) for h in range(8)], axis=0
            ).astype(jnp.bfloat16)
            fresh_key = rotate(field(x, 2048 + 128 * side)).astype(jnp.bfloat16)
            fresh_values.append(field(x, 2304 + 128 * side))
            cached.append(
                jnp.where(
                    second_row[:64],
                    times_transposed(query, key_ref[1, :, columns]),
                    times_transposed(query, key_ref[0, :, columns]),
                )
            )
            fresh.append(times_transposed(query, fresh_key))
        scores = jnp.where(live, jnp.concatenate(cached, axis=0) * scale, -jnp.inf)
        fresh_scores = jnp.where(fresh_live, jnp.concatenate(fresh, axis=0) * scale, -jnp.inf)
        highest = jnp.maximum(
            jnp.max(scores, axis=-1, keepdims=True), jnp.max(fresh_scores, axis=-1, keepdims=True)
        )
        weight = jnp.exp(scores - highest)
        fresh_weight = jnp.exp(fresh_scores - highest)
        inverse = 1.0 / (
            jnp.sum(weight, axis=-1, keepdims=True) + jnp.sum(fresh_weight, axis=-1, keepdims=True)
        )
        prob = weight * inverse
        fresh_prob = (fresh_weight * inverse).astype(jnp.bfloat16)
        columns = slice(x * 256, (x + 1) * 256)
        attended = (
            jnp.dot(
                jnp.where(second_row, 0.0, prob).astype(jnp.bfloat16),
                value_ref[0, :, columns],
                preferred_element_type=jnp.float32,
            )
            + jnp.dot(
                jnp.where(second_row, prob, 0.0).astype(jnp.bfloat16),
                value_ref[1, :, columns],
                preferred_element_type=jnp.float32,
            )
            + jnp.dot(
                fresh_prob,
                jnp.concatenate(fresh_values, axis=1).astype(jnp.bfloat16),
                preferred_element_type=jnp.float32,
            )
        )
        for h in range(0, 16, 2):
            natural = 8 * x + h // 2
            y = (natural >> 1) & 3
            start = pl.multiple_of(place_ref[natural] * 256, 256)
            side = slice(128 * (h // 8), 128 * (h // 8) + 128)
            block = jnp.concatenate(
                [attended[8 * h : 8 * h + 8, side], attended[8 * h + 8 : 8 * h + 16, side]], axis=1
            ).astype(jnp.bfloat16)
            for copy in range(4):
                out_ref[4 * y + copy, 0, :, pl.ds(start, 256)] = block


def attention(fields, cosine, sine, keys, values, lengths, places):
    table = pl.BlockSpec((1, 8, HEAD_SIZE), lambda i, *_: (i, 0, 0))
    cache = pl.BlockSpec((2, CONTEXT_SLOTS, KEY_WIDTH), lambda i, *_: (i, 0, 0))
    return pl.pallas_call(
        attention_kernel,
        out_shape=jax.ShapeDtypeStruct((16, PAIRS, 8, 2048), jnp.bfloat16),
        grid_spec=pltpu.PrefetchScalarGridSpec(
            num_scalar_prefetch=2,
            grid=(PAIRS,),
            in_specs=[
                pl.BlockSpec((16, 1, 8, 2560), lambda i, *_: (0, i, 0, 0)),
                table,
                table,
                cache,
                cache,
            ],
            out_specs=pl.BlockSpec((16, 1, 8, 2048), lambda i, *_: (0, i, 0, 0)),
        ),
        compiler_params=pltpu.CompilerParams(vmem_limit_bytes=VMEM_LIMIT),
        cost_estimate=pl.CostEstimate(
            flops=PAIRS * 8 * 8 * 64 * 512 * 128,
            bytes_accessed=PAIRS * 4 * 1024 * 1024,
            transcendentals=PAIRS * 8 * 64 * 512,
        ),
        name="attention",
    )(lengths, places, fields, cosine, sine, keys, values)


def product_kernel(starts, rows_ref, *refs):
    pieces, out_ref = refs[:-1], refs[-1]
    total = None
    for start, piece in zip(starts, pieces):
        term = jnp.dot(
            rows_ref[:, start : start + piece.shape[0]],
            piece[...],
            preferred_element_type=jnp.float32,
        )
        total = term if total is None else total + term
    out_ref[...] = total.astype(jnp.bfloat16).reshape(out_ref.shape)


def product(rows, pieces, by_block, name):
    starts = tuple(start for start, _ in pieces)
    weights = [weight for _, weight in pieces]
    count, depth = rows.shape
    columns = weights[0].shape[1]
    blocks = columns // 256
    if by_block:
        out_shape, out_spec = (blocks, count, 256), pl.BlockSpec((1, count, 256), lambda i: (i, 0, 0))
    else:
        out_shape, out_spec = (count, columns), pl.BlockSpec((count, 256), lambda i: (0, i))
    return pl.pallas_call(
        functools.partial(product_kernel, starts),
        out_shape=jax.ShapeDtypeStruct(out_shape, jnp.bfloat16),
        grid=(blocks,),
        in_specs=[pl.BlockSpec((count, depth), lambda i: (0, 0))]
        + [pl.BlockSpec((weight.shape[0], 256), lambda i: (0, i)) for weight in weights],
        out_specs=out_spec,
        compiler_params=pltpu.CompilerParams(vmem_limit_bytes=VMEM_LIMIT),
        cost_estimate=pl.CostEstimate(
            flops=2 * count * depth * columns,
            bytes_accessed=2 * depth * (count + columns),
            transcendentals=0,
        ),
        name=name,
    )(rows, *weights)


def depth_pieces(own, above, below, far):
    depth = own.shape[0]
    half = far[0].shape[0]
    pieces = []
    for start, weight in (
        (0, own),
        (2 * depth, above),
        (6 * depth, below),
        (4 * depth, far[0]),
        (4 * depth + half, far[1]),
    ):
        pieces += [(start, weight), (start + depth, swap_cores(weight))]
    return pieces


def block_places():
    z_index = lax.axis_index("zh") * 2 + lax.axis_index("zl")
    natural = jnp.arange(32, dtype=jnp.int32)
    zl, c, y, zh = natural >> 4, (natural >> 3) & 1, (natural >> 1) & 3, natural & 1
    plane = (zh * 2 + zl - z_index + 4) & 3
    core = (c - lax.axis_index("c") + 2) & 1
    return (plane * 2 + core) * 4 + y


def body(
    hidden_states,
    norm_gain,
    lengths,
    rotated_key_cache,
    value_cache,
    qkv_weight,
    qkv_grad,
    qkv_first,
    qkv_second,
    out_weight,
    out_grad,
    out_first,
    out_second,
):
    depth = qkv_weight.shape[0]

    places = block_places() >> 2
    qkv_updated = adam_step(qkv_weight, qkv_grad, qkv_first, qkv_second)
    qkv_piece = jnp.concatenate(
        [
            qkv_updated[:, :QUERY_WIDTH].reshape(depth, 4, 2048),
            qkv_updated[:, QUERY_WIDTH : QUERY_WIDTH + KEY_WIDTH].reshape(depth, 4, 256),
            qkv_updated[:, QUERY_WIDTH + KEY_WIDTH :].reshape(depth, 4, 256),
        ],
        axis=2,
    ).transpose(1, 0, 2)
    qkv_own = lax.all_to_all(qkv_piece, "x", split_axis=0, concat_axis=0, tiled=True)
    qkv_own = qkv_own.reshape(4 * depth, 2560)
    normed = norm_rows(hidden_states, norm_gain, places)
    out_updated = adam_step(out_weight, out_grad, out_first, out_second)
    out_piece = out_updated.reshape(depth, 8, 4, 256).transpose(2, 0, 1, 3).reshape(4, depth, 2048)
    qkv_own, normed, out_piece = lax.optimization_barrier((qkv_own, normed, out_piece))

    half = qkv_own.shape[0] // 2
    below = shift_z(qkv_own, 1)
    above = shift_z(qkv_own, -1)
    normed_rows = lax.all_to_all(normed, PLANE, split_axis=0, concat_axis=0, tiled=True)
    below, above, normed_rows = lax.optimization_barrier((below, above, normed_rows))
    far = shift_z(below[:half], 1), shift_z(above[half:], -1)
    out_piece, _ = lax.optimization_barrier((out_piece, normed_rows))
    out_own = lax.all_to_all(out_piece, "x", split_axis=0, concat_axis=0, tiled=True)
    out_own = out_own.reshape(4 * depth, 2048)
    cosine, sine = rotary_tables(lengths)
    far, out_own, cosine, sine = lax.optimization_barrier((far, out_own, cosine, sine))
    out_below = shift_z(out_own, 1)
    out_above = shift_z(out_own, -1)

    projected = product(
        normed_rows.reshape(-1, 2048), depth_pieces(qkv_own, above, below, far), False, "qkv_partial"
    )
    fields = lax.all_to_all(
        projected.reshape(16, -1, 2560), PLANE, split_axis=0, concat_axis=0, tiled=True
    )

    fields, out_below, out_above = lax.optimization_barrier((fields, out_below, out_above))
    out_far = shift_z(out_below[:half], 1), shift_z(out_above[half:], -1)
    attended = attention(
        fields.reshape(16, PAIRS, 8, 2560),
        cosine,
        sine,
        rotated_key_cache,
        value_cache,
        lengths,
        places,
    )
    attended, out_far = lax.optimization_barrier((attended, out_far))
    attended = lax.all_to_all(attended, PLANE, split_axis=0, concat_axis=0, tiled=True)
    partial = product(
        attended.reshape(-1, 2048),
        depth_pieces(out_own, out_above, out_below, out_far),
        True,
        "out_partial",
    )
    partial = lax.all_to_all(partial, ("y", "zh"), split_axis=0, concat_axis=0, tiled=True)
    total = jnp.sum(partial.reshape(4, 2, -1, 256).astype(jnp.float32), axis=0)
    total = total.astype(jnp.bfloat16).reshape(2, 4, 4, -1, DECODE_STEPS, 256)
    return total.transpose(4, 1, 0, 2, 3, 5).reshape(DECODE_STEPS, -1, 256)


def solution(mesh):
    every = ("zl", "c", "y", "zh", "x")
    fine = jax.sharding.Mesh(mesh.devices.reshape(2, 2, 4, 2, 4), every)
    return jax.shard_map(
        body,
        mesh=fine,
        in_specs=(
            P(None, every, None),
            P(),
            P(every),
            P(every, None, None),
            P(every, None, None),
        )
        + (P(every, None),) * 8,
        out_specs=P(None, ("zl", "c"), ("y", "zh", "x")),
        check_vma=False,
    )
```

time: 320 us -> 228 us (0.71)
  blocking collectives: 100 us -> 23 us
  waiting for transfers between devices: 133 us -> 99.5 us
  starting transfers between devices: 11.5 us -> 43 us
  Pallas kernels: 21.1 us -> 36.6 us
  matrix products: 14.7 us -> 0 us
  between operations: 13.7 us -> 0.32 us
    all_gather x2 -> x0, waiting for transfers between devices: 98.7 us -> none  [the longest x1 98.7 us: body(): out_owned = lax.all_gather(out_own, ('zl', 'c', 'zh'), axis=0, tiled=True)]
    all_to_all x3 -> x0, blocking collectives: 73.2 us -> none  [the longest x1 33.5 us: body(): lax.all_to_all(qkv_piece, PLANE, split_axis=0, concat_axis=0, tiled=True)]
    ppermute x4 -> x8, waiting for transfers between devices: 34.7 us -> 67.1 us  [shift_z(): lax.ppermute(value, ('zl', 'zh'), [(position(z), position(z + step + Z_SI...]
    all_to_all x0 -> x4, waiting for transfers between devices: none -> 23.7 us  [the longest x1 12.5 us: body(): lax.all_to_all(attended, PLANE, split_axis=0, concat_axis=0, tiled=True)]
    all_to_all x0 -> x4, starting transfers between devices: none -> 22.3 us  [the longest x1 7.31 us: body(): lax.all_to_all(projected.reshape(16, -1, 2560), PLANE, split_axis=0, conc...]
    pallas_call x2 -> x3, Pallas kernels: 7.77 us -> 24.8 us  [the longest x2 22.3 us: product(): pl.pallas_call(functools.partial(product_kernel, starts), out_shape=jax.S...]
    dot_general x8 -> x0, matrix products: 14.7 us -> none  [body(): jnp.dot(normed_rows[:, start:start + 1024], part, preferred_element_type=...]
    ppermute x4 -> x10, waiting for transfers between devices: 0.01 us -> 8.77 us  [swap_cores(): return lax.ppermute(value, 'c', [(0, 1), (1, 0)])]
  transfers between devices with their start and end apart: 11 -> 23, of which waited for: 4 -> 12; matrix products, arithmetic and copies ran while one was open for 9% -> 5% of each run, Pallas kernels for 4% -> 6%
where the time goes in v1:
time: 228 us; the launch traced here: 227 us
  waiting for transfers between devices  99.5 us (44%)
  starting transfers between devices  43 us (19%)
  Pallas kernels  36.6 us (16%)
  blocking collectives  23 us (10%)
  local copies, waits for them, and re-layouts  14 us (6%)
  other arithmetic  10.7 us (5%)
    ppermute x8, waiting for transfers between devices, shift_z(): lax.ppermute(value, ('zl', 'zh'), [(position(z), position(z + step + Z_SI...  67.1 us
    all_to_all x1, blocking collectives, body(): lax.all_to_all(partial, ('y', 'zh'), split_axis=0, concat_axis=0, tiled=T...  23 us
    pallas_call x2, Pallas kernels, product(): pl.pallas_call(functools.partial(product_kernel, starts), out_shape=jax.S...  22.3 us
    ppermute x8, starting transfers between devices, shift_z(): lax.ppermute(value, ('zl', 'zh'), [(position(z), position(z + step + Z_SI...  13.9 us
    all_to_all x1, waiting for transfers between devices, body(): lax.all_to_all(attended, PLANE, split_axis=0, concat_axis=0, tiled=True)  12.5 us
    pallas_call x1, Pallas kernels, attention(): pl.pallas_call(attention_kernel, out_shape=jax.ShapeDtypeStruct((16, PAIR...  11.7 us
    all_to_all x1, waiting for transfers between devices, body(): lax.all_to_all(qkv_piece, 'x', split_axis=0, concat_axis=0, tiled=True)  9.46 us
    ppermute x10, waiting for transfers between devices, swap_cores(): return lax.ppermute(value, 'c', [(0, 1), (1, 0)])  8.77 us
  transfers between devices with their start and end apart: 23, of which 12 were waited for; matrix products, arithmetic and copies ran while one was open for 5% of the time, Pallas kernels for 6%

profile of v1, /device:TPU:0, one launch (start us, length us, event | category | flops | bytes accessed | tf_op | source)
XLA Modules:
  0.0 227.1 jit_solution(8240575514393811068)
XLA Ops:
  0.0 4.8 %fusion.2 = bf16[64,10240]{1,0:T(8,128)(2,1)S(1)} fusion(bf16[64,10240]{1,0:T(8,128)(2,1)} %param.18, bf16[64,10240]{1,0:T(8,128)(2,1)} %param.19, bf16[64,10240]{1,0:T(8,128)(2,1)} %param.21, bf16[64,10240]{1,0:T(8,128)(2,1)} %param.20), kind=kLoop, calls=%fused_computation.10 | loop fusion | flops 13107200 | bytes 6553600 | tf_op jit(solution)/shard_map/convert_element_type | solution.py:43
  5.1 1.2 maximum_bitcast_fusion
  6.3 4.4 %all-to-all-start = ((bf16[4,64,2560]{2,1,0:T(8,128)(2,1)}), bf16[4,64,2560]{2,1,0:T(8,128)(2,1)}, u32[]{:S(2)}, u32[]{:S(2)}) async-start(bf16[4,64,2560]{2,1,0:T(8,128)(2,1)} %maximum_bitcast_fusion), calls=%async_computation | async-start | bytes 2621440 | tf_op jit(solution)/shard_map/all_to_all | solution.py:319
  10.7 3.5 %fusion.12 = bf16[64,8192]{1,0:T(8,128)(2,1)S(1)} fusion(bf16[64,8192]{1,0:T(8,128)(2,1)S(1)} %copy-done.4, bf16[64,8192]{1,0:T(8,128)(2,1)S(1)} %copy-done.5, bf16[64,8192]{1,0:T(8,128)(2,1)} %param.25, bf16[64,8192]{1,0:T(8,128)(2,1)} %param.24), kind=kLoop, calls=%fused_computation.20 | loop fusion | flops 10485760 | bytes 5242880 | tf_op jit(solution)/shard_map/convert_element_type | solution.py:43
  14.4 0.8 reshape.88
  15.4 1.3 reshape.89
  16.7 2.5 %norm_rows.1 = bf16[16,24,2048]{2,1,0:T(8,128)(2,1)} custom-call(s32[32]{0:T(128)S(1)} %fusion.30.place_ref, bf16[4,6,8192]{2,1,0:T(8,128)(2,1)S(1)} %copy.29.hidden_ref, bf16[1,8192]{1,0:T(2,128)(2,1)S(1)} %broadcast_in_dim.2.gain_ref), custom_call_target="tpu_custom_call" | custom-call | tf_op jit(solution)/shard_map/norm_rows/pallas_call | solution.py:85
  19.2 9.5 %all-to-all-done = bf16[4,64,2560]{2,1,0:T(8,128)(2,1)} async-done(((bf16[4,64,2560]{2,1,0:T(8,128)(2,1)}), bf16[4,64,2560]{2,1,0:T(8,128)(2,1)}, u32[]{:S(2)}, u32[]{:S(2)}) %all-to-all-start) | async-done | bytes 1310752 | tf_op jit(solution)/shard_map/all_to_all | solution.py:319
  28.7 5.5 %all-to-all-start.1 = ((bf16[16,24,2048]{2,1,0:T(8,128)(2,1)}), bf16[16,24,2048]{2,1,0:T(8,128)(2,1)S(1)}, u32[]{:S(2)}, u32[]{:S(2)}) async-start(bf16[16,24,2048]{2,1,0:T(8,128)(2,1)} %norm_rows.1), calls=%async_computation.1 | async-start | bytes 3145728 | tf_op jit(solution)/shard_map/all_to_all | solution.py:329
  34.2 2.0 collective-permute-start
  36.2 2.2 collective-permute-start.1
  38.4 27.8 %collective-permute-done.refs_4_ = bf16[256,2560]{1,0:T(8,128)(2,1)} collective-permute-done((bf16[256,2560]{1,0:T(8,128)(2,1)}, bf16[256,2560]{1,0:T(8,128)(2,1)}, u32[]{:S(2)}, u32[]{:S(2)}) %collective-permute-start) | collective-permute-done | bytes 1310752 | tf_op jit(solution)/shard_map/ppermute | solution.py:56
  66.2 4.4 %all-to-all-start.2 = ((bf16[4,64,2048]{2,1,0:T(8,128)(2,1)}), bf16[4,64,2048]{2,1,0:T(8,128)(2,1)S(1)}, u32[]{:S(2)}, u32[]{:S(2)}) async-start(bf16[4,64,2048]{2,1,0:T(8,128)(2,1)} %reshape.89), calls=%async_computation.2 | async-start | bytes 2097152 | tf_op jit(solution)/shard_map/all_to_all | solution.py:333
  70.9 1.1 slice.25
  72.0 0.6 collective-permute-start.3
  72.6 1.1 slice.24
  73.9 1.3 collective-permute-start.5
  75.2 2.0 collective-permute-start.6
  77.3 0.7 pad_maximum_fusion
  78.0 14.3 %collective-permute-done.5.refs_6_ = bf16[128,2560]{1,0:T(8,128)(2,1)S(1)} collective-permute-done((bf16[128,2560]{1,0:T(8,128)(2,1)S(1)}, bf16[128,2560]{1,0:T(8,128)(2,1)S(1)}, u32[]{:S(2)}, u32[]{:S(2)}) %collective-permute-start.5) | collective-permute-done | bytes 655392 | tf_op jit(solution)/shard_map/ppermute | solution.py:56
  92.4 0.5 collective-permute-start.8
  92.9 1.6 collective-permute-done.7.refs_7_
  94.5 0.9 collective-permute-done.8.refs_9_
  95.4 0.8 copy-done.16
  96.3 12.2 %qkv_partial.1 = bf16[384,2560]{1,0:T(8,128)(2,1)} custom-call(bf16[384,2048]{1,0:T(8,128)(2,1)} %bitcast.32, bf16[256,2560]{1,0:T(8,128)(2,1)} %bitcast.1.refs_0_, bf16[256,2560]{1,0:T(8,128)(2,1)} %collective-permute-done.2.refs_1_, bf16[256,2560]{1,0:T(8,128)(2,1)} %collective-permute-done.1.refs_2_, bf16[256,2560]{1,0:T(8,128)(2,1)} %collective-permute-done.3.refs_3_, ...), custom_call_target="tpu_custom_call" | custom-call | flops 4026531840 | bytes 12058624 | tf_op jit(solution)/shard_map/qkv_partial/pallas_call | solution.py:251
  108.4 7.3 %all-to-all-start.3 = ((bf16[16,24,2560]{2,1,0:T(8,128)(2,1)}), bf16[16,24,2560]{2,1,0:T(8,128)(2,1)S(1)}, u32[]{:S(2)}, u32[]{:S(2)}) async-start(bf16[16,24,2560]{2,1,0:T(8,128)(2,1)} %bitcast.31), calls=%async_computation.3 | async-start | bytes 3932160 | tf_op jit(solution)/shard_map/all_to_all | solution.py:343
  115.7 3.0 %collective-permute-start.10 = (bf16[256,2048]{1,0:T(8,128)(2,1)S(1)}, bf16[256,2048]{1,0:T(8,128)(2,1)S(1)}, u32[]{:S(2)}, u32[]{:S(2)}) collective-permute-start(bf16[256,2048]{1,0:T(8,128)(2,1)S(1)} %bitcast.36), channel_id=1, source_target_pairs={{0,68},{64,0},{4,64},{68,4},{1,69},{65,1},{5,65},{69,5},{2,70},{66... | collective-permute-start | bytes 3145736 | tf_op jit(solution)/shard_map/ppermute | solution.py:56
  118.8 22.4 %collective-permute-done.10.refs_2_ = bf16[256,2048]{1,0:T(8,128)(2,1)S(1)} collective-permute-done((bf16[256,2048]{1,0:T(8,128)(2,1)S(1)}, bf16[256,2048]{1,0:T(8,128)(2,1)S(1)}, u32[]{:S(2)}, u32[]{:S(2)}) %collective-permute-start.10) | collective-permute-done | bytes 1048608 | tf_op jit(solution)/shard_map/ppermute | solution.py:56
  141.2 1.0 copy-done.8
  142.2 2.6 %collective-permute-done.9.refs_4_ = bf16[256,2048]{1,0:T(8,128)(2,1)} collective-permute-done((bf16[256,2048]{1,0:T(8,128)(2,1)S(1)}, bf16[256,2048]{1,0:T(8,128)(2,1)}, u32[]{:S(2)}, u32[]{:S(2)}) %collective-permute-start.9) | collective-permute-done | bytes 1048608 | tf_op jit(solution)/shard_map/ppermute | solution.py:56
  144.7 1.8 all-to-all-done.3
  146.5 1.4 slice.26
  147.9 1.4 collective-permute-start.11
  149.3 1.1 slice.27
  150.4 2.0 collective-permute-start.12
  152.4 11.7 %attention.1 = bf16[16,3,8,2048]{3,2,1,0:T(8,128)(2,1)} custom-call(s32[6]{0:T(128)} %lengths_ref.1, s32[32]{0:T(128)} %copy-done, bf16[16,3,8,2560]{3,2,1,0:T(8,128)(2,1)} %bitcast.26, f32[3,8,128]{2,1,0:T(8,128)} %get-tuple-element.34.cos_ref, f32[3,8,128]{2,1,0:T(8,128)} %get-tuple-element.35.sin_ref, bf16[6,512,1024]{2,1,0:T(8,128)(2,1)} %key_ref.1, ...), custom_call_target="tpu_custom_call" | custom-call | flops 805306368 | bytes 12582912 | tf_op jit(solution)/shard_map/attention/pallas_call | solution.py:203
  164.1 5.1 %all-to-all-start.4 = ((bf16[16,3,8,2048]{3,2,1,0:T(8,128)(2,1)}), bf16[16,3,8,2048]{3,2,1,0:T(8,128)(2,1)S(1)}, u32[]{:S(2)}, u32[]{:S(2)}) async-start(bf16[16,3,8,2048]{3,2,1,0:T(8,128)(2,1)} %attention.1), calls=%async_computation.4 | async-start | bytes 3145728 | tf_op jit(solution)/shard_map/all_to_all | solution.py:359
  169.3 0.5 collective-permute-start.14
  170.5 2.1 collective-permute-done.13.refs_1_
  172.6 2.2 collective-permute-done.16.refs_7_
  174.8 1.9 collective-permute-done.17.refs_9_
  176.7 0.8 copy-done.19
  177.5 1.0 copy-done.12
  178.5 12.5 %all-to-all-done.4 = bf16[16,3,8,2048]{3,2,1,0:T(8,128)(2,1)S(1)} async-done(((bf16[16,3,8,2048]{3,2,1,0:T(8,128)(2,1)}), bf16[16,3,8,2048]{3,2,1,0:T(8,128)(2,1)S(1)}, u32[]{:S(2)}, u32[]{:S(2)}) %all-to-all-start.4) | async-done | bytes 1572896 | tf_op jit(solution)/shard_map/all_to_all | solution.py:359
  191.0 1.2 copy-done.3
  192.2 10.2 %out_partial.1 = bf16[8,384,256]{2,1,0:T(8,128)(2,1)} custom-call(bf16[384,2048]{1,0:T(8,128)(2,1)} %bitcast.33, bf16[256,2048]{1,0:T(8,128)(2,1)} %bitcast.39, bf16[256,2048]{1,0:T(8,128)(2,1)} %copy-done.11, bf16[256,2048]{1,0:T(8,128)(2,1)} %copy-done.8, bf16[256,2048]{1,0:T(8,128)(2,1)} %copy-done.12, bf16[256,2048]{1,0:T(8,128)(2,1)} %collective-permute-done.9.refs_4_, ...), custom_call_target="tpu_custom_call" | custom-call | flops 3221225472 | bytes 9961472 | tf_op jit(solution)/shard_map/out_partial/pallas_call | solution.py:251
  202.3 23.0 %all_to_all.30 = bf16[8,384,256]{2,1,0:T(8,128)(2,1)S(1)} all-to-all(bf16[8,384,256]{2,1,0:T(8,128)(2,1)} %out_partial.1), channel_id=1, replica_groups=mesh['zl'=2,'c'=2,'y'=4,'zh'=2,'x'=4] {'y','zh'}, dimensions={0} | all-to-all | bytes 3145728 | tf_op jit(solution)/shard_map/all_to_all | solution.py:366
  226.3 0.8 copy.33
  (73 shorter events, 3.1 us)
Async XLA Ops:
  5.1 5.6 %copy-start.4 = (bf16[64,8192]{1,0:T(8,128)(2,1)S(1)}, bf16[64,8192]{1,0:T(8,128)(2,1)}, u32[]{:S(2)}) copy-start(bf16[64,8192]{1,0:T(8,128)(2,1)} %param.22) | copy-start | bytes 3145732
  5.1 5.6 %copy-start.5 = (bf16[64,8192]{1,0:T(8,128)(2,1)S(1)}, bf16[64,8192]{1,0:T(8,128)(2,1)}, u32[]{:S(2)}) copy-start(bf16[64,8192]{1,0:T(8,128)(2,1)} %param.23) | copy-start | bytes 3145732
  6.3 22.4 %all-to-all-start = ((bf16[4,64,2560]{2,1,0:T(8,128)(2,1)}), bf16[4,64,2560]{2,1,0:T(8,128)(2,1)}, u32[]{:S(2)}, u32[]{:S(2)}) async-start(bf16[4,64,2560]{2,1,0:T(8,128)(2,1)} %maximum_bitcast_fusion), calls=%async_computation | async-start | bytes 2621440 | tf_op jit(solution)/shard_map/all_to_all | solution.py:319
  10.6 3.5 %copy-start.7 = (bf16[4,6,8192]{2,0,1:T(4,128)(2,1)S(1)}, bf16[4,6,8192]{2,0,1:T(4,128)(2,1)}, u32[]{:S(2)}) copy-start(bf16[4,6,8192]{2,0,1:T(4,128)(2,1)} %param.13) | copy-start | bytes 1179652
  10.6 3.7 %copy-start.9 = (bf16[8192]{0:T(1024)(128)(2,1)S(1)}, bf16[8192]{0:T(1024)(128)(2,1)}, u32[]{:S(2)}) copy-start(bf16[8192]{0:T(1024)(128)(2,1)} %param.14) | copy-start | bytes 49156
  16.7 12.0 %copy-start = (s32[32]{0:T(128)}, s32[32]{0:T(128)S(1)}, u32[]{:S(2)}) copy-start(s32[32]{0:T(128)S(1)} %fusion.30.place_ref) | copy-start | bytes 388
  28.7 41.9 %copy-start.10 = (s32[6]{0:T(128)S(1)}, s32[6]{0:T(128)}, u32[]{:S(2)}) copy-start(s32[6]{0:T(128)} %lengths_ref.1) | copy-start | bytes 76
  28.7 37.5 %all-to-all-start.1 = ((bf16[16,24,2048]{2,1,0:T(8,128)(2,1)}), bf16[16,24,2048]{2,1,0:T(8,128)(2,1)S(1)}, u32[]{:S(2)}, u32[]{:S(2)}) async-start(bf16[16,24,2048]{2,1,0:T(8,128)(2,1)} %norm_rows.1), calls=%async_computation.1 | async-start | bytes 3145728 | tf_op jit(solution)/shard_map/all_to_all | solution.py:329
  34.2 32.0 %collective-permute-start = (bf16[256,2560]{1,0:T(8,128)(2,1)}, bf16[256,2560]{1,0:T(8,128)(2,1)}, u32[]{:S(2)}, u32[]{:S(2)}) collective-permute-start(bf16[256,2560]{1,0:T(8,128)(2,1)} %bitcast.1.refs_0_), channel_id=1, source_target_pairs={{0,64},{64,4},{4,68},{68,0},{1,65},{65,5},{5,69},{69,1},{2,66},{66... | collective-permute-start | bytes 3932168 | tf_op jit(solution)/shard_map/ppermute | solution.py:56
  36.2 30.0 %collective-permute-start.1 = (bf16[256,2560]{1,0:T(8,128)(2,1)}, bf16[256,2560]{1,0:T(8,128)(2,1)}, u32[]{:S(2)}, u32[]{:S(2)}) collective-permute-start(bf16[256,2560]{1,0:T(8,128)(2,1)} %bitcast.1.refs_0_), channel_id=1, source_target_pairs={{0,68},{64,0},{4,64},{68,4},{1,69},{65,1},{5,65},{69,5},{2,70},{66... | collective-permute-start | bytes 3932168 | tf_op jit(solution)/shard_map/ppermute | solution.py:56
  66.2 7.6 %copy-start.2 = (bf16[16,24,2048]{2,1,0:T(8,128)(2,1)}, bf16[16,24,2048]{2,1,0:T(8,128)(2,1)S(1)}, u32[]{:S(2)}) copy-start(bf16[16,24,2048]{2,1,0:T(8,128)(2,1)S(1)} %all-to-all-done.1) | copy-start | bytes 4718596
  66.2 26.1 %all-to-all-start.2 = ((bf16[4,64,2048]{2,1,0:T(8,128)(2,1)}), bf16[4,64,2048]{2,1,0:T(8,128)(2,1)S(1)}, u32[]{:S(2)}, u32[]{:S(2)}) async-start(bf16[4,64,2048]{2,1,0:T(8,128)(2,1)} %reshape.89), calls=%async_computation.2 | async-start | bytes 2097152 | tf_op jit(solution)/shard_map/all_to_all | solution.py:333
  70.9 22.0 %collective-permute-start.2 = (bf16[256,2560]{1,0:T(8,128)(2,1)}, bf16[256,2560]{1,0:T(8,128)(2,1)}, u32[]{:S(2)}, u32[]{:S(2)}) collective-permute-start(bf16[256,2560]{1,0:T(8,128)(2,1)} %bitcast.1.refs_0_), channel_id=1, source_target_pairs={{0,32},{32,0},{1,33},{33,1},{2,34},{34,2},{3,35},{35,3},{4,36},{36... | collective-permute-start | bytes 3932168 | tf_op jit(solution)/shard_map/ppermute | solution.py:62
  72.0 20.8 %collective-permute-start.3 = (bf16[256,2560]{1,0:T(8,128)(2,1)}, bf16[256,2560]{1,0:T(8,128)(2,1)}, u32[]{:S(2)}, u32[]{:S(2)}) collective-permute-start(bf16[256,2560]{1,0:T(8,128)(2,1)} %collective-permute-done.1.refs_2_), channel_id=1, source_target_pairs={{0,32},{32,0},{1,33},{33,1},{2,34},{34,2},{3,35},{35,3},{4,36},{36... | collective-permute-start | bytes 3932168 | tf_op jit(solution)/shard_map/ppermute | solution.py:62
  73.8 19.1 %collective-permute-start.4 = (bf16[256,2560]{1,0:T(8,128)(2,1)}, bf16[256,2560]{1,0:T(8,128)(2,1)}, u32[]{:S(2)}, u32[]{:S(2)}) collective-permute-start(bf16[256,2560]{1,0:T(8,128)(2,1)} %collective-permute-done.refs_4_), channel_id=1, source_target_pairs={{0,32},{32,0},{1,33},{33,1},{2,34},{34,2},{3,35},{35,3},{4,36},{36... | collective-permute-start | bytes 3932168 | tf_op jit(solution)/shard_map/ppermute | solution.py:62
  73.9 18.4 %collective-permute-start.5 = (bf16[128,2560]{1,0:T(8,128)(2,1)S(1)}, bf16[128,2560]{1,0:T(8,128)(2,1)S(1)}, u32[]{:S(2)}, u32[]{:S(2)}) collective-permute-start(bf16[128,2560]{1,0:T(8,128)(2,1)S(1)} %slice.24), channel_id=1, source_target_pairs={{0,64},{64,4},{4,68},{68,0},{1,65},{65,5},{5,69},{69,1},{2,66},{66... | collective-permute-start | bytes 1966088 | tf_op jit(solution)/shard_map/ppermute | solution.py:56
  75.2 17.1 %collective-permute-start.6 = (bf16[128,2560]{1,0:T(8,128)(2,1)S(1)}, bf16[128,2560]{1,0:T(8,128)(2,1)S(1)}, u32[]{:S(2)}, u32[]{:S(2)}) collective-permute-start(bf16[128,2560]{1,0:T(8,128)(2,1)S(1)} %slice.25), channel_id=1, source_target_pairs={{0,68},{64,0},{4,64},{68,4},{1,69},{65,1},{5,65},{69,5},{2,70},{66... | collective-permute-start | bytes 1966088 | tf_op jit(solution)/shard_map/ppermute | solution.py:56
  92.3 3.1 %copy-start.13 = (bf16[128,2560]{1,0:T(8,128)(2,1)}, bf16[128,2560]{1,0:T(8,128)(2,1)S(1)}, u32[]{:S(2)}) copy-start(bf16[128,2560]{1,0:T(8,128)(2,1)S(1)} %collective-permute-done.5.refs_6_) | copy-start | bytes 1966084
  92.3 3.1 %copy-start.14 = (bf16[128,2560]{1,0:T(8,128)(2,1)}, bf16[128,2560]{1,0:T(8,128)(2,1)S(1)}, u32[]{:S(2)}) copy-start(bf16[128,2560]{1,0:T(8,128)(2,1)S(1)} %collective-permute-done.6.refs_8_) | copy-start | bytes 1966084
  92.3 77.0 %copy-start.6 = (bf16[4,64,2048]{2,1,0:T(8,128)(2,1)}, bf16[4,64,2048]{2,1,0:T(8,128)(2,1)S(1)}, u32[]{:S(2)}) copy-start(bf16[4,64,2048]{2,1,0:T(8,128)(2,1)S(1)} %all-to-all-done.2) | copy-start | bytes 3145732
  92.3 2.2 collective-permute-start.7
  92.4 3.0 %collective-permute-start.8 = (bf16[128,2560]{1,0:T(8,128)(2,1)S(1)}, bf16[128,2560]{1,0:T(8,128)(2,1)S(1)}, u32[]{:S(2)}, u32[]{:S(2)}) collective-permute-start(bf16[128,2560]{1,0:T(8,128)(2,1)S(1)} %collective-permute-done.6.refs_8_), channel_id=1, source_target_pairs={{0,32},{32,0},{1,33},{33,1},{2,34},{34,2},{3,35},{35,3},{4,36},{36... | collective-permute-start | bytes 1966088 | tf_op jit(solution)/shard_map/ppermute | solution.py:62
  94.5 0.9 copy-start.15
  95.4 0.9 copy-start.16
  108.4 38.0 %all-to-all-start.3 = ((bf16[16,24,2560]{2,1,0:T(8,128)(2,1)}), bf16[16,24,2560]{2,1,0:T(8,128)(2,1)S(1)}, u32[]{:S(2)}, u32[]{:S(2)}) async-start(bf16[16,24,2560]{2,1,0:T(8,128)(2,1)} %bitcast.31), calls=%async_computation.3 | async-start | bytes 3932160 | tf_op jit(solution)/shard_map/all_to_all | solution.py:343
  115.7 25.4 %collective-permute-start.10 = (bf16[256,2048]{1,0:T(8,128)(2,1)S(1)}, bf16[256,2048]{1,0:T(8,128)(2,1)S(1)}, u32[]{:S(2)}, u32[]{:S(2)}) collective-permute-start(bf16[256,2048]{1,0:T(8,128)(2,1)S(1)} %bitcast.36), channel_id=1, source_target_pairs={{0,68},{64,0},{4,64},{68,4},{1,69},{65,1},{5,65},{69,5},{2,70},{66... | collective-permute-start | bytes 3145736 | tf_op jit(solution)/shard_map/ppermute | solution.py:56
  118.8 26.0 %collective-permute-start.9 = (bf16[256,2048]{1,0:T(8,128)(2,1)S(1)}, bf16[256,2048]{1,0:T(8,128)(2,1)}, u32[]{:S(2)}, u32[]{:S(2)}) collective-permute-start(bf16[256,2048]{1,0:T(8,128)(2,1)S(1)} %bitcast.37), channel_id=1, source_target_pairs={{0,64},{64,4},{4,68},{68,0},{1,65},{65,5},{5,69},{69,1},{2,66},{66... | collective-permute-start | bytes 3145736 | tf_op jit(solution)/shard_map/ppermute | solution.py:56
  141.2 1.0 copy-start.8
  146.5 5.9 %copy-start.1 = (bf16[16,24,2560]{2,1,0:T(8,128)(2,1)}, bf16[16,24,2560]{2,1,0:T(8,128)(2,1)S(1)}, u32[]{:S(2)}) copy-start(bf16[16,24,2560]{2,1,0:T(8,128)(2,1)S(1)} %all-to-all-done.3) | copy-start | bytes 5898244
  147.9 16.2 %collective-permute-start.11 = (bf16[128,2048]{1,0:T(8,128)(2,1)S(1)}, bf16[128,2048]{1,0:T(8,128)(2,1)S(1)}, u32[]{:S(2)}, u32[]{:S(2)}) collective-permute-start(bf16[128,2048]{1,0:T(8,128)(2,1)S(1)} %slice.26), channel_id=1, source_target_pairs={{0,64},{64,4},{4,68},{68,0},{1,65},{65,5},{5,69},{69,1},{2,66},{66... | collective-permute-start | bytes 1572872 | tf_op jit(solution)/shard_map/ppermute | solution.py:56
  150.4 13.7 %collective-permute-start.12 = (bf16[128,2048]{1,0:T(8,128)(2,1)S(1)}, bf16[128,2048]{1,0:T(8,128)(2,1)}, u32[]{:S(2)}, u32[]{:S(2)}) collective-permute-start(bf16[128,2048]{1,0:T(8,128)(2,1)S(1)} %slice.27), channel_id=1, source_target_pairs={{0,68},{64,0},{4,64},{68,4},{1,69},{65,1},{5,65},{69,5},{2,70},{66... | collective-permute-start | bytes 1572872 | tf_op jit(solution)/shard_map/ppermute | solution.py:56
  164.1 26.9 %copy-start.17 = (bf16[128,2048]{1,0:T(8,128)(2,1)}, bf16[128,2048]{1,0:T(8,128)(2,1)S(1)}, u32[]{:S(2)}) copy-start(bf16[128,2048]{1,0:T(8,128)(2,1)S(1)} %collective-permute-done.11.refs_6_) | copy-start | bytes 1572868
  164.1 26.9 %all-to-all-start.4 = ((bf16[16,3,8,2048]{3,2,1,0:T(8,128)(2,1)}), bf16[16,3,8,2048]{3,2,1,0:T(8,128)(2,1)S(1)}, u32[]{:S(2)}, u32[]{:S(2)}) async-start(bf16[16,3,8,2048]{3,2,1,0:T(8,128)(2,1)} %attention.1), calls=%async_computation.4 | async-start | bytes 3145728 | tf_op jit(solution)/shard_map/all_to_all | solution.py:359
  169.3 3.3 %collective-permute-start.13 = (bf16[256,2048]{1,0:T(8,128)(2,1)S(1)}, bf16[256,2048]{1,0:T(8,128)(2,1)S(1)}, u32[]{:S(2)}, u32[]{:S(2)}) collective-permute-start(bf16[256,2048]{1,0:T(8,128)(2,1)S(1)} %bitcast.38), channel_id=1, source_target_pairs={{0,32},{32,0},{1,33},{33,1},{2,34},{34,2},{3,35},{35,3},{4,36},{36... | collective-permute-start | bytes 3145736 | tf_op jit(solution)/shard_map/ppermute | solution.py:62
  169.3 7.4 %collective-permute-start.14 = (bf16[256,2048]{1,0:T(8,128)(2,1)}, bf16[256,2048]{1,0:T(8,128)(2,1)S(1)}, u32[]{:S(2)}, u32[]{:S(2)}) collective-permute-start(bf16[256,2048]{1,0:T(8,128)(2,1)} %copy-done.8), channel_id=1, source_target_pairs={{0,32},{32,0},{1,33},{33,1},{2,34},{34,2},{3,35},{35,3},{4,36},{36... | collective-permute-start | bytes 3145736 | tf_op jit(solution)/shard_map/ppermute | solution.py:62
  169.8 8.7 %collective-permute-start.15 = (bf16[256,2048]{1,0:T(8,128)(2,1)}, bf16[256,2048]{1,0:T(8,128)(2,1)}, u32[]{:S(2)}, u32[]{:S(2)}) collective-permute-start(bf16[256,2048]{1,0:T(8,128)(2,1)} %collective-permute-done.9.refs_4_), channel_id=1, source_target_pairs={{0,32},{32,0},{1,33},{33,1},{2,34},{34,2},{3,35},{35,3},{4,36},{36... | collective-permute-start | bytes 3145736 | tf_op jit(solution)/shard_map/ppermute | solution.py:62
  169.9 4.9 %collective-permute-start.16 = (bf16[128,2048]{1,0:T(8,128)(2,1)S(1)}, bf16[128,2048]{1,0:T(8,128)(2,1)S(1)}, u32[]{:S(2)}, u32[]{:S(2)}) collective-permute-start(bf16[128,2048]{1,0:T(8,128)(2,1)S(1)} %collective-permute-done.11.refs_6_), channel_id=1, source_target_pairs={{0,32},{32,0},{1,33},{33,1},{2,34},{34,2},{3,35},{35,3},{4,36},{36... | collective-permute-start | bytes 1572872 | tf_op jit(solution)/shard_map/ppermute | solution.py:62
  170.4 6.3 %collective-permute-start.17 = (bf16[128,2048]{1,0:T(8,128)(2,1)}, bf16[128,2048]{1,0:T(8,128)(2,1)S(1)}, u32[]{:S(2)}, u32[]{:S(2)}) collective-permute-start(bf16[128,2048]{1,0:T(8,128)(2,1)} %collective-permute-done.12.refs_8_), channel_id=1, source_target_pairs={{0,32},{32,0},{1,33},{33,1},{2,34},{34,2},{3,35},{35,3},{4,36},{36... | collective-permute-start | bytes 1572872 | tf_op jit(solution)/shard_map/ppermute | solution.py:62
  172.6 4.1 %copy-start.11 = (bf16[256,2048]{1,0:T(8,128)(2,1)}, bf16[256,2048]{1,0:T(8,128)(2,1)S(1)}, u32[]{:S(2)}) copy-start(bf16[256,2048]{1,0:T(8,128)(2,1)S(1)} %collective-permute-done.13.refs_1_) | copy-start | bytes 3145732
  174.8 1.9 copy-start.18
  176.7 0.8 copy-start.19
  177.5 1.0 copy-start.12
  191.0 1.2 copy-start.3

commit v2 on v1

v2 whole, which is shorter than its diff:
```python
import functools
import math

import jax
import jax.numpy as jnp
from jax import lax
from jax.experimental import pallas as pl
from jax.experimental.pallas import tpu as pltpu
from jax.sharding import PartitionSpec as P

D = 8192
HQ = 64
KEY_HEADS = 8
HEAD_SIZE = 128
CONTEXT_SLOTS = 512
DECODE_STEPS = 4
QUERY_WIDTH = 8192
KEY_WIDTH = 1024


learn_rate = 0.008
beta_one = 0.9
beta_two = 0.95
bias_one = 1.0 - beta_one * beta_one
bias_two = 1.0 - beta_two * beta_two
adam_eps = 1e-08
decay_rate = 0.1
rope_base = 500000.0
norm_eps = 1e-05


def adam_step(weight, gradient, moment_one, moment_two):
    grad_wide = gradient.astype(jnp.float32)
    first_new = beta_one * moment_one.astype(jnp.float32) + (1.0 - beta_one) * grad_wide
    second_new = (
        beta_two * moment_two.astype(jnp.float32) + (1.0 - beta_two) * grad_wide * grad_wide
    )
    weight_wide = weight.astype(jnp.float32)
    update = (
        first_new / bias_one / (jnp.sqrt(second_new / bias_two) + adam_eps)
        + decay_rate * weight_wide
    )
    return (weight_wide - learn_rate * update).astype(jnp.bfloat16)


PAIRS = 3
Z_SIZE = 4
PLANE = ("y", "x")
VMEM_LIMIT = 56 * 1024 * 1024


def shift_z(value, step):
    def position(z):
        return (z % 2) * 2 + (z // 2) % 2

    return lax.ppermute(
        value, ("zl", "zh"), [(position(z), position(z + step + Z_SIZE)) for z in range(Z_SIZE)]
    )


def swap_cores(value):
    return lax.ppermute(value, "c", [(0, 1), (1, 0)])


def joint_adam_kernel(*refs):
    out_ref = refs[-1]
    query, key, value = (
        adam_step(*(ref[...] for ref in refs[part:12:3])) for part in range(3)
    )
    for x in range(2):
        out_ref[x, :, :1024] = query[:, x * 1024 : (x + 1) * 1024]
        out_ref[x, :, 1024:1152] = key[:, x * 128 : (x + 1) * 128]
        out_ref[x, :, 1152:] = value[:, x * 128 : (x + 1) * 128]


def joint_adam(half, *arrays):
    depth = arrays[0].shape[0]
    specs = [
        pl.BlockSpec((depth, 2048), lambda i: (0, 2 * half + i)),
        pl.BlockSpec((depth, 256), lambda i: (0, 32 + 2 * half + i)),
        pl.BlockSpec((depth, 256), lambda i: (0, 36 + 2 * half + i)),
    ]
    return pl.pallas_call(
        joint_adam_kernel,
        out_shape=jax.ShapeDtypeStruct((4, depth, 1280), jnp.bfloat16),
        grid=(2,),
        in_specs=specs * 4,
        out_specs=pl.BlockSpec((2, depth, 1280), lambda i: (i, 0, 0)),
        compiler_params=pltpu.CompilerParams(vmem_limit_bytes=VMEM_LIMIT),
        name="joint_adam",
    )(*(array for array in arrays for _ in range(3)))


def norm_kernel(hidden_ref, gain_ref, out_ref, scratch_ref):
    gain = gain_ref[...].astype(jnp.float32)
    rows = hidden_ref.shape[1]
    for step in range(DECODE_STEPS):
        wide = hidden_ref[step].astype(jnp.float32)
        inverse = lax.rsqrt(jnp.mean(wide * wide, axis=-1, keepdims=True) + norm_eps)
        normed = wide * inverse * gain
        for row in range(rows):
            at = row * DECODE_STEPS + step
            scratch_ref[at : at + 1, :] = normed[row : row + 1]
    for natural in range(D // 256):
        start = ((natural >> 3) * 2 + (natural & 1)) * 256
        block = scratch_ref[:, natural * 256 : (natural + 1) * 256].astype(jnp.bfloat16)
        for x in range(4):
            out_ref[4 * ((natural >> 1) & 3) + x, :, start : start + 256] = block


def norm_rows(hidden_states, norm_gain):
    rows = DECODE_STEPS * hidden_states.shape[1]
    vmem = pl.BlockSpec(memory_space=pltpu.VMEM)
    return pl.pallas_call(
        norm_kernel,
        out_shape=jax.ShapeDtypeStruct((16, rows, D // 4), jnp.bfloat16),
        in_specs=[vmem, vmem],
        out_specs=vmem,
        scratch_shapes=[pltpu.VMEM((rows, D), jnp.float32)],
        compiler_params=pltpu.CompilerParams(vmem_limit_bytes=16 * 1024 * 1024),
        name="norm_rows",
    )(hidden_states, norm_gain[None])


def rotary_tables(lengths):
    half_width = HEAD_SIZE // 2
    frequency = jnp.power(
        rope_base, -2.0 * jnp.arange(half_width, dtype=jnp.float32) / HEAD_SIZE
    )
    positions = lengths[:, None] + jnp.arange(DECODE_STEPS, dtype=jnp.int32)[None, :]
    angles = positions.astype(jnp.float32)[..., None] * frequency
    cosine, sine = jnp.cos(angles), jnp.sin(angles)
    shape = (PAIRS, 8, HEAD_SIZE)
    return (
        jnp.concatenate([cosine, cosine], axis=-1).reshape(shape),
        jnp.concatenate([-sine, sine], axis=-1).reshape(shape),
    )


def attention_kernel(
    lengths_ref, field_ref, cos_ref, sin_ref, key_ref, value_ref, *refs
):
    out_ref = refs[-1]
    pair = pl.program_id(0)
    cosine, sine = cos_ref[0], sin_ref[0]
    scale = 1.0 / math.sqrt(HEAD_SIZE)
    line = lax.broadcasted_iota(jnp.int32, (128, 1), 0)
    second_row = ((line >> 2) & 1) == 1
    step = line & 3
    length = jnp.where(second_row, lengths_ref[2 * pair + 1], lengths_ref[2 * pair])
    live = lax.broadcasted_iota(jnp.int32, (128, CONTEXT_SLOTS), 1) < length
    fresh_column = lax.broadcasted_iota(jnp.int32, (128, 8), 1)
    fresh_live = (((fresh_column >> 2) & 1) == ((line >> 2) & 1)) & ((fresh_column & 3) <= step)

    def field(x, start):
        total = None
        for y in range(4):
            term = field_ref[4 * y + x, 0, :, start : start + 128].astype(jnp.float32)
            total = term if total is None else total + term
        return total.astype(jnp.bfloat16).astype(jnp.float32)

    def rotate(vector):
        return vector * cosine + pltpu.roll(vector, 64, 1) * sine

    def times_transposed(left, right):
        return lax.dot_general(
            left, right, (((1,), (1,)), ((), ())), preferred_element_type=jnp.float32
        )

    for first in range(0, KEY_HEADS // 2, 2):
        cached, fresh, fresh_values = [], [], []
        for kv in (first, first + 1):
            columns = slice(kv * HEAD_SIZE, (kv + 1) * HEAD_SIZE)
            query = jnp.concatenate(
                [rotate(field(kv, h * 128)) for h in range(8)], axis=0
            ).astype(jnp.bfloat16)
            fresh_key = rotate(field(kv, 1024)).astype(jnp.bfloat16)
            fresh_values.append(field(kv, 1152))
            cached.append(
                jnp.where(
                    second_row[:64],
                    times_transposed(query, key_ref[1, :, columns]),
                    times_transposed(query, key_ref[0, :, columns]),
                )
            )
            fresh.append(times_transposed(query, fresh_key))
        scores = jnp.where(live, jnp.concatenate(cached, axis=0) * scale, -jnp.inf)
        fresh_scores = jnp.where(fresh_live, jnp.concatenate(fresh, axis=0) * scale, -jnp.inf)
        highest = jnp.maximum(
            jnp.max(scores, axis=-1, keepdims=True), jnp.max(fresh_scores, axis=-1, keepdims=True)
        )
        weight = jnp.exp(scores - highest)
        fresh_weight = jnp.exp(fresh_scores - highest)
        inverse = 1.0 / (
            jnp.sum(weight, axis=-1, keepdims=True) + jnp.sum(fresh_weight, axis=-1, keepdims=True)
        )
        prob = weight * inverse
        fresh_prob = (fresh_weight * inverse).astype(jnp.bfloat16)
        columns = slice(first * 128, first * 128 + 256)
        attended = (
            jnp.dot(
                jnp.where(second_row, 0.0, prob).astype(jnp.bfloat16),
                value_ref[0, :, columns],
                preferred_element_type=jnp.float32,
            )
            + jnp.dot(
                jnp.where(second_row, prob, 0.0).astype(jnp.bfloat16),
                value_ref[1, :, columns],
                preferred_element_type=jnp.float32,
            )
            + jnp.dot(
                fresh_prob,
                jnp.concatenate(fresh_values, axis=1).astype(jnp.bfloat16),
                preferred_element_type=jnp.float32,
            )
        )
        for h in range(0, 16, 2):
            natural = 4 * first + h // 2
            y = (natural >> 1) & 3
            start = ((natural >> 3) * 2 + (natural & 1)) * 256
            side = slice(128 * (h // 8), 128 * (h // 8) + 128)
            block = jnp.concatenate(
                [attended[8 * h : 8 * h + 8, side], attended[8 * h + 8 : 8 * h + 16, side]], axis=1
            ).astype(jnp.bfloat16)
            for copy in range(4):
                out_ref[4 * y + copy, 0, :, start : start + 256] = block


def attention(half, fields, cosine, sine, keys, values, lengths, *before):
    table = pl.BlockSpec((1, 8, HEAD_SIZE), lambda i, *_: (i, 0, 0))
    cache = pl.BlockSpec((2, CONTEXT_SLOTS, KEY_WIDTH // 2), lambda i, *_: (i, 0, half))
    return pl.pallas_call(
        attention_kernel,
        out_shape=jax.ShapeDtypeStruct((16, PAIRS, 8, 2048), jnp.bfloat16),
        grid_spec=pltpu.PrefetchScalarGridSpec(
            num_scalar_prefetch=1,
            grid=(PAIRS,),
            in_specs=[
                pl.BlockSpec((16, 1, 8, 1280), lambda i, *_: (0, i, 0, 0)),
                table,
                table,
                cache,
                cache,
            ]
            + [pl.BlockSpec(memory_space=pl.ANY)] * len(before),
            out_specs=pl.BlockSpec((16, 1, 8, 1024), lambda i, *_: (0, i, 0, half)),
        ),
        input_output_aliases={6: 0} if before else {},
        compiler_params=pltpu.CompilerParams(vmem_limit_bytes=VMEM_LIMIT),
        cost_estimate=pl.CostEstimate(
            flops=PAIRS * 4 * 8 * 64 * 512 * 128,
            bytes_accessed=PAIRS * 2 * 1024 * 1024,
            transcendentals=PAIRS * 4 * 64 * 512,
        ),
        name="attention",
    )(lengths, fields, cosine, sine, keys, values, *before)


def product_kernel(parts, places, by_block, start_ref, *refs):
    rows, pieces = refs[:parts], refs[parts : parts + len(places)]
    out_ref, rows_held, held, row_sems, piece_sems = refs[parts + len(places) :]
    width = rows[0].shape[1]
    row_copies = [
        pltpu.make_async_copy(part, rows_held.at[:, pl.ds(i * width, width)], row_sems.at[i])
        for i, part in enumerate(rows)
    ]
    for copy in row_copies:
        copy.start()

    blocks, columns = held.shape[0], held.shape[2]

    def copies(block):
        for i, (piece, (index, offset)) in enumerate(zip(pieces, places)):
            start = pl.multiple_of(start_ref[index] + offset, 128)
            yield pltpu.make_async_copy(
                piece.at[:, pl.ds(block * columns, columns)],
                held.at[block, pl.ds(start, piece.shape[0]), :],
                piece_sems.at[block, i],
            )

    for block in range(blocks):
        for copy in copies(block):
            copy.start()
    for copy in row_copies:
        copy.wait()
    for block in range(blocks):
        for copy in copies(block):
            copy.wait()
        for part in range(columns // 256):
            result = jnp.dot(
                rows_held[...],
                held[block, :, part * 256 : (part + 1) * 256],
                preferred_element_type=jnp.float32,
            ).astype(jnp.bfloat16)
            at = block * (columns // 256) + part
            if by_block:
                out_ref[at] = result
            else:
                out_ref[:, at * 256 : (at + 1) * 256] = result


def product(rows, pieces, starts, turns, by_block, name):
    places = tuple(place for place, _ in pieces)
    weights = [weight for _, weight in pieces]
    count, depth = rows[0].shape[0], sum(part.shape[1] for part in rows)
    columns = weights[0].shape[1]
    blocks = columns // 256
    anywhere = pl.BlockSpec(memory_space=pl.ANY)
    return pl.pallas_call(
        functools.partial(product_kernel, len(rows), places, by_block),
        out_shape=jax.ShapeDtypeStruct(
            (blocks, count, 256) if by_block else (count, columns), jnp.bfloat16
        ),
        in_specs=[pl.BlockSpec(memory_space=pltpu.SMEM)] + [anywhere] * (len(rows) + len(weights)),
        out_specs=pl.BlockSpec(memory_space=pltpu.VMEM),
        scratch_shapes=[
            pltpu.VMEM((count, depth), jnp.bfloat16),
            pltpu.VMEM((turns, depth, columns // turns), jnp.bfloat16),
            pltpu.SemaphoreType.DMA((len(rows),)),
            pltpu.SemaphoreType.DMA((turns, len(weights))),
        ],
        compiler_params=pltpu.CompilerParams(vmem_limit_bytes=VMEM_LIMIT),
        cost_estimate=pl.CostEstimate(
            flops=2 * count * depth * columns,
            bytes_accessed=2 * depth * (count + columns),
            transcendentals=0,
        ),
        name=name,
    )(starts, *rows, *weights)


def piece_starts(size):
    ahead = jnp.arange(8, dtype=jnp.int32)
    plane = (lax.axis_index("zh") * 2 + lax.axis_index("zl") + (ahead >> 1)) & 3
    core = (lax.axis_index("c") + ahead) & 1
    return ((plane & 1) * 4 + core * 2 + (plane >> 1)) * size


def both_cores(*pieces):
    result = []
    for plane, offset, own, other in pieces:
        result += [((2 * plane, offset), own), ((2 * plane + 1, offset), other)]
    return result


def body(
    hidden_states,
    norm_gain,
    lengths,
    rotated_key_cache,
    value_cache,
    qkv_weight,
    qkv_grad,
    qkv_first,
    qkv_second,
    out_weight,
    out_grad,
    out_first,
    out_second,
):
    depth = qkv_weight.shape[0]
    barrier = lax.optimization_barrier

    def to_owner(piece):
        piece = lax.all_to_all(piece, "x", split_axis=0, concat_axis=0, tiled=True)
        return piece.reshape(4 * depth, -1)

    joint = qkv_weight, qkv_grad, qkv_first, qkv_second
    own_one = to_owner(joint_adam(0, *joint))
    piece_two = joint_adam(1, *joint)
    normed = norm_rows(hidden_states, norm_gain)
    own_one, piece_two, normed = barrier((own_one, piece_two, normed))

    below_one, above_one = shift_z(own_one, 1), shift_z(own_one, -1)
    own_one_swapped = swap_cores(own_one)
    own_two = to_owner(piece_two)
    normed, own_two = barrier((normed, own_two))
    normed_rows = lax.all_to_all(normed, PLANE, split_axis=0, concat_axis=0, tiled=True)
    out_updated = adam_step(out_weight, out_grad, out_first, out_second)
    out_piece = out_updated.reshape(depth, 8, 4, 256).transpose(2, 0, 1, 3).reshape(4, depth, 2048)
    cosine, sine = rotary_tables(lengths)
    starts = piece_starts(4 * depth)
    below_one, above_one, own_two, own_one_swapped = barrier(
        (below_one, above_one, own_two, own_one_swapped)
    )
    far_one, above_two = shift_z(below_one, 1), shift_z(own_two, -1)
    above_one_swapped, below_one_swapped = swap_cores(above_one), swap_cores(below_one)
    own_two_swapped = swap_cores(own_two)
    far_one, above_two, own_two, above_one_swapped, below_one_swapped, own_two_swapped = barrier(
        (far_one, above_two, own_two, above_one_swapped, below_one_swapped, own_two_swapped)
    )
    normed_rows, out_piece, cosine, sine, starts = barrier(
        (normed_rows, out_piece, cosine, sine, starts)
    )
    out_own = to_owner(out_piece)

    rows = [normed_rows.reshape(-1, 2048)]
    pieces = both_cores(
        (0, 0, own_one, own_one_swapped),
        (1, 0, above_one, above_one_swapped),
        (3, 0, below_one, below_one_swapped),
        (2, 0, far_one, swap_cores(far_one)),
    )
    projected_one = product(rows, pieces, starts, 1, False, "qkv_partial_one")
    projected_one, own_two, above_two = barrier((projected_one, own_two, above_two))
    below_two, far_two = shift_z(own_two, 1), shift_z(above_two, -1)
    above_two_swapped = swap_cores(above_two)
    projected_one = projected_one.reshape(16, -1, 1280)
    fields_one = lax.all_to_all(projected_one, PLANE, split_axis=0, concat_axis=0, tiled=True)
    pieces = both_cores(
        (0, 0, own_two, own_two_swapped),
        (1, 0, above_two, above_two_swapped),
        (3, 0, below_two, swap_cores(below_two)),
        (2, 0, far_two, swap_cores(far_two)),
    )
    projected_two = product(rows, pieces, starts, 1, False, "qkv_partial_two")
    projected_two = projected_two.reshape(16, -1, 1280)
    projected_two, fields_one, out_own = barrier((projected_two, fields_one, out_own))
    out_below, out_above = shift_z(out_own, 1), shift_z(out_own, -1)
    out_own_swapped = swap_cores(out_own)
    fields_two = lax.all_to_all(projected_two, PLANE, split_axis=0, concat_axis=0, tiled=True)

    caches = rotated_key_cache, value_cache, lengths
    fields_shape = (16, PAIRS, 8, 1280)
    attended = attention(0, fields_one.reshape(fields_shape), cosine, sine, *caches)
    fields_two, attended, out_below, out_above, out_own_swapped = barrier(
        (fields_two, attended, out_below, out_above, out_own_swapped)
    )
    half = out_own.shape[0] // 2
    out_far = shift_z(out_below[:half], 1), shift_z(out_above[half:], -1)
    out_below_swapped, out_above_swapped = swap_cores(out_below), swap_cores(out_above)
    attended = attention(1, fields_two.reshape(fields_shape), cosine, sine, *caches, attended)
    attended, out_far, out_below_swapped, out_above_swapped = barrier(
        (attended, out_far, out_below_swapped, out_above_swapped)
    )
    attended = lax.all_to_all(attended, PLANE, split_axis=0, concat_axis=0, tiled=True)
    pieces = both_cores(
        (0, 0, out_own, out_own_swapped),
        (1, 0, out_above, out_above_swapped),
        (3, 0, out_below, out_below_swapped),
        (2, 0, out_far[0], swap_cores(out_far[0])),
        (2, half, out_far[1], swap_cores(out_far[1])),
    )
    rows = [attended.reshape(-1, 2048)]
    partial = product(rows, pieces, starts, 2, True, "out_partial")
    partial = lax.all_to_all(partial, ("y", "zh"), split_axis=0, concat_axis=0, tiled=True)
    total = jnp.sum(partial.reshape(4, 2, -1, 256).astype(jnp.float32), axis=0)
    total = total.astype(jnp.bfloat16).reshape(2, 4, 4, -1, DECODE_STEPS, 256)
    return total.transpose(4, 1, 0, 2, 3, 5).reshape(DECODE_STEPS, -1, 256)


def solution(mesh):
    every = ("zl", "c", "y", "zh", "x")
    fine = jax.sharding.Mesh(mesh.devices.reshape(2, 2, 4, 2, 4), every)
    return jax.shard_map(
        body,
        mesh=fine,
        in_specs=(
            P(None, every, None),
            P(),
            P(every),
            P(every, None, None),
            P(every, None, None),
        )
        + (P(every, None),) * 8,
        out_specs=P(None, ("zl", "c"), ("y", "zh", "x")),
        check_vma=False,
    )
```

time: 228 us -> 218 us (0.956)
  waiting for transfers between devices: 99.5 us -> 65.3 us
  blocking collectives: 23 us -> 37.1 us
  Pallas kernels: 36.6 us -> 47.2 us
  starting transfers between devices: 43 us -> 49.5 us
  other arithmetic: 10.7 us -> 5.85 us
  local copies, waits for them, and re-layouts: 14 us -> 11.1 us
    ppermute x8 -> x10, waiting for transfers between devices: 67.1 us -> 20.5 us  [shift_z(): lax.ppermute(value, ('zl', 'zh'), [(position(z), position(z + step + Z_SI...]
    all_to_all x0 -> x1, blocking collectives: none -> 13.9 us  [to_owner(): piece = lax.all_to_all(piece, 'x', split_axis=0, concat_axis=0, tiled=True)]
    all_to_all x1, waiting for transfers between devices: 12.5 us -> 20 us  [body(): lax.all_to_all(attended, PLANE, split_axis=0, concat_axis=0, tiled=True)]
    pallas_call x2 -> x5, Pallas kernels: 22.3 us -> 29.8 us  [the longest x3 23.2 us: product(): pl.pallas_call(functools.partial(product_kernel, len(rows), places, by_bl...]
    all_to_all x3 -> x4, waiting for transfers between devices: 11.2 us -> 16.5 us  [the longest x1 9.24 us: body(): lax.all_to_all(projected_two, PLANE, split_axis=0, concat_axis=0, tiled=T...]
    convert_element_type x2 -> x1, other arithmetic: 8.29 us -> 4.04 us  [adam_step(): return (weight_wide - learn_rate * update).astype(jnp.bfloat16)]
    ppermute x10 -> x13, waiting for transfers between devices: 8.77 us -> 4.81 us  [swap_cores(): return lax.ppermute(value, 'c', [(0, 1), (1, 0)])]
    pallas_call x1 -> x2, Pallas kernels: 11.7 us -> 15.5 us  [attention(): pl.pallas_call(attention_kernel, out_shape=jax.ShapeDtypeStruct((16, PAIR...]
  transfers between devices with their start and end apart: 23 -> 29, of which waited for: 12 -> 15; matrix products, arithmetic and copies ran while one was open for 5% -> 5% of each run, Pallas kernels for 6% -> 16%
where the time goes in v2:
time: 218 us; the launch traced here: 216 us
  waiting for transfers between devices  65.3 us (30%)
  starting transfers between devices  49.5 us (23%)
  Pallas kernels  47.2 us (22%)
  blocking collectives  37.1 us (17%)
  local copies, waits for them, and re-layouts  11.1 us (5%)
  other arithmetic  5.85 us (3%)
    pallas_call x3, Pallas kernels, product(): pl.pallas_call(functools.partial(product_kernel, len(rows), places, by_bl...  23.2 us
    all_to_all x1, blocking collectives, body(): lax.all_to_all(partial, ('y', 'zh'), split_axis=0, concat_axis=0, tiled=T...  23.1 us
    ppermute x10, waiting for transfers between devices, shift_z(): lax.ppermute(value, ('zl', 'zh'), [(position(z), position(z + step + Z_SI...  20.5 us
    all_to_all x1, waiting for transfers between devices, body(): lax.all_to_all(attended, PLANE, split_axis=0, concat_axis=0, tiled=True)  20 us
    ppermute x10, starting transfers between devices, shift_z(): lax.ppermute(value, ('zl', 'zh'), [(position(z), position(z + step + Z_SI...  16.2 us
    pallas_call x2, Pallas kernels, attention(): pl.pallas_call(attention_kernel, out_shape=jax.ShapeDtypeStruct((16, PAIR...  15.5 us
    all_to_all x1, blocking collectives, to_owner(): piece = lax.all_to_all(piece, 'x', split_axis=0, concat_axis=0, tiled=True)  13.9 us
    all_to_all x1, waiting for transfers between devices, body(): lax.all_to_all(projected_two, PLANE, split_axis=0, concat_axis=0, tiled=T...  9.24 us
  transfers between devices with their start and end apart: 29, of which 15 were waited for; matrix products, arithmetic and copies ran while one was open for 5% of the time, Pallas kernels for 16%

profile of v2, /device:TPU:0, one launch (start us, length us, event | category | flops | bytes accessed | tf_op | source)
XLA Modules:
  0.0 216.3 jit_solution(9679304504573026146)
XLA Ops:
  0.0 3.3 %joint_adam.2 = bf16[4,64,1280]{2,1,0:T(8,128)(2,1)} custom-call(bf16[64,10240]{1,0:T(8,128)(2,1)} %refs_2_.3, bf16[64,10240]{1,0:T(8,128)(2,1)} %refs_2_.3, bf16[64,10240]{1,0:T(8,128)(2,1)} %refs_2_.3, bf16[64,10240]{1,0:T(8,128)(2,1)} %refs_5_.3, bf16[64,10240]{1,0:T(8,128)(2,1)} %refs_5_.3, bf16[64,10240]{1,0:T(8,128)(2,1)} %refs_5_.3, ...), custom_call_target="tpu_custom_call" | custom-call | tf_op jit(solution)/shard_map/joint_adam/pallas_call | solution.py:83
  3.3 4.4 %all-to-all-start = ((bf16[4,64,1280]{2,1,0:T(8,128)(2,1)}), bf16[4,64,1280]{2,1,0:T(8,128)(2,1)S(1)}, u32[]{:S(2)}, u32[]{:S(2)}) async-start(bf16[4,64,1280]{2,1,0:T(8,128)(2,1)} %joint_adam.2), calls=%async_computation | async-start | bytes 1310720 | tf_op jit(solution)/shard_map/all_to_all | solution.py:365
  7.7 3.3 %joint_adam.3 = bf16[4,64,1280]{2,1,0:T(8,128)(2,1)} custom-call(bf16[64,10240]{1,0:T(8,128)(2,1)} %refs_2_.3, bf16[64,10240]{1,0:T(8,128)(2,1)} %refs_2_.3, bf16[64,10240]{1,0:T(8,128)(2,1)} %refs_2_.3, bf16[64,10240]{1,0:T(8,128)(2,1)} %refs_5_.3, bf16[64,10240]{1,0:T(8,128)(2,1)} %refs_5_.3, bf16[64,10240]{1,0:T(8,128)(2,1)} %refs_5_.3, ...), custom_call_target="tpu_custom_call" | custom-call | tf_op jit(solution)/shard_map/joint_adam/pallas_call | solution.py:83
  11.3 1.9 norm_rows.1
  13.2 5.4 %all-to-all-done = bf16[4,64,1280]{2,1,0:T(8,128)(2,1)S(1)} async-done(((bf16[4,64,1280]{2,1,0:T(8,128)(2,1)}), bf16[4,64,1280]{2,1,0:T(8,128)(2,1)S(1)}, u32[]{:S(2)}, u32[]{:S(2)}) %all-to-all-start) | async-done | bytes 655392 | tf_op jit(solution)/shard_map/all_to_all | solution.py:365
  18.6 4.0 %collective-permute-start.1 = (bf16[256,1280]{1,0:T(8,128)(2,1)S(1)}, bf16[256,1280]{1,0:T(8,128)(2,1)}, u32[]{:S(2)}, u32[]{:S(2)}) collective-permute-start(bf16[256,1280]{1,0:T(8,128)(2,1)S(1)} %bitcast.30), channel_id=1, source_target_pairs={{0,68},{64,0},{4,64},{68,4},{1,69},{65,1},{5,65},{69,5},{2,70},{66... | collective-permute-start | bytes 1966088 | tf_op jit(solution)/shard_map/ppermute | solution.py:56
  22.6 13.9 %all_to_all.40 = bf16[4,64,1280]{2,1,0:T(8,128)(2,1)S(1)} all-to-all(bf16[4,64,1280]{2,1,0:T(8,128)(2,1)S(1)} %copy-done.3), channel_id=1, replica_groups=mesh['zl'=2,'c'=2,'y'=4,'zh'=2,'x'=4] {'x'}, dimensions={0} | all-to-all | bytes 1310720 | tf_op jit(solution)/shard_map/all_to_all | solution.py:365
  36.6 5.2 %all-to-all-start.2 = ((bf16[16,24,2048]{2,1,0:T(8,128)(2,1)}), bf16[16,24,2048]{2,1,0:T(8,128)(2,1)S(1)}, u32[]{:S(2)}, u32[]{:S(2)}) async-start(bf16[16,24,2048]{2,1,0:T(8,128)(2,1)} %norm_rows.1), calls=%async_computation.2 | async-start | bytes 3145728 | tf_op jit(solution)/shard_map/all_to_all | solution.py:378
  42.4 3.0 %collective-permute-start.4 = (bf16[256,1280]{1,0:T(8,128)(2,1)S(1)}, bf16[256,1280]{1,0:T(8,128)(2,1)}, u32[]{:S(2)}, u32[]{:S(2)}) collective-permute-start(bf16[256,1280]{1,0:T(8,128)(2,1)S(1)} %bitcast.26), channel_id=1, source_target_pairs={{0,68},{64,0},{4,64},{68,4},{1,69},{65,1},{5,65},{69,5},{2,70},{66... | collective-permute-start | bytes 1966088 | tf_op jit(solution)/shard_map/ppermute | solution.py:56
  45.4 4.0 %fusion.2 = bf16[64,8192]{1,0:T(8,128)(2,1)S(1)} fusion(bf16[64,8192]{1,0:T(8,128)(2,1)} %param.22, bf16[64,8192]{1,0:T(8,128)(2,1)} %param.23, bf16[64,8192]{1,0:T(8,128)(2,1)} %param.25, bf16[64,8192]{1,0:T(8,128)(2,1)} %param.24), kind=kLoop, calls=%fused_computation.6 | loop fusion | flops 10485760 | bytes 5242880 | tf_op jit(solution)/shard_map/convert_element_type | solution.py:43
  49.8 1.6 reshape.86
  51.4 1.4 copy.22
  52.8 1.3 reshape.87
  54.1 6.5 %collective-permute-done.3.refs_7_ = bf16[256,1280]{1,0:T(8,128)(2,1)} collective-permute-done((bf16[256,1280]{1,0:T(8,128)(2,1)}, bf16[256,1280]{1,0:T(8,128)(2,1)}, u32[]{:S(2)}, u32[]{:S(2)}) %collective-permute-start.3) | collective-permute-done | bytes 655392 | tf_op jit(solution)/shard_map/ppermute | solution.py:56
  60.6 0.6 add_multiply_fusion.start_ref
  61.3 0.7 pad_maximum_fusion
  62.0 3.4 %all-to-all-done.2 = bf16[16,24,2048]{2,1,0:T(8,128)(2,1)S(1)} async-done(((bf16[16,24,2048]{2,1,0:T(8,128)(2,1)}), bf16[16,24,2048]{2,1,0:T(8,128)(2,1)S(1)}, u32[]{:S(2)}, u32[]{:S(2)}) %all-to-all-start.2) | async-done | bytes 1572896 | tf_op jit(solution)/shard_map/all_to_all | solution.py:378
  65.4 4.2 %all-to-all-start.4 = ((bf16[4,64,2048]{2,1,0:T(8,128)(2,1)}), bf16[4,64,2048]{2,1,0:T(8,128)(2,1)}, u32[]{:S(2)}, u32[]{:S(2)}) async-start(bf16[4,64,2048]{2,1,0:T(8,128)(2,1)} %reshape.87), calls=%async_computation.4 | async-start | bytes 2097152 | tf_op jit(solution)/shard_map/all_to_all | solution.py:365
  69.7 0.8 copy-done.9
  70.5 6.8 %qkv_partial_one.1 = bf16[384,1280]{1,0:T(8,128)(2,1)} custom-call(s32[8]{0:T(128)} %add_multiply_fusion.start_ref, bf16[384,2048]{1,0:T(8,128)(2,1)} %bitcast.17, bf16[256,1280]{1,0:T(8,128)(2,1)} %bitcast.32, bf16[256,1280]{1,0:T(8,128)(2,1)} %collective-permute-done.2.refs_2_, bf16[256,1280]{1,0:T(8,128)(2,1)} %collective-permute-done.1.refs_3_, ...), custom_call_target="tpu_custom_call" | custom-call | flops 2013265920 | bytes 6815744 | tf_op jit(solution)/shard_map/qkv_partial_one/pallas_call | solution.py:309
  77.4 3.2 %collective-permute-start.12 = (bf16[256,1280]{1,0:T(8,128)(2,1)}, bf16[256,1280]{1,0:T(8,128)(2,1)S(1)}, u32[]{:S(2)}, u32[]{:S(2)}) collective-permute-start(bf16[256,1280]{1,0:T(8,128)(2,1)} %collective-permute-done.4.refs_3_), channel_id=1, source_target_pairs={{0,68},{64,0},{4,64},{68,4},{1,69},{65,1},{5,65},{69,5},{2,70},{66... | collective-permute-start | bytes 1966088 | tf_op jit(solution)/shard_map/ppermute | solution.py:56
  80.7 1.9 all-to-all-done.4
  82.5 5.2 %all-to-all-start.3 = ((bf16[16,24,1280]{2,1,0:T(8,128)(2,1)}), bf16[16,24,1280]{2,1,0:T(8,128)(2,1)S(1)}, u32[]{:S(2)}, u32[]{:S(2)}) async-start(bf16[16,24,1280]{2,1,0:T(8,128)(2,1)} %bitcast.22), calls=%async_computation.3 | async-start | bytes 1966080 | tf_op jit(solution)/shard_map/all_to_all | solution.py:409
  87.8 4.8 %collective-permute-done.10.refs_5_ = bf16[256,1280]{1,0:T(8,128)(2,1)S(1)} collective-permute-done((bf16[256,1280]{1,0:T(8,128)(2,1)S(1)}, bf16[256,1280]{1,0:T(8,128)(2,1)S(1)}, u32[]{:S(2)}, u32[]{:S(2)}) %collective-permute-start.10) | collective-permute-done | bytes 655392 | tf_op jit(solution)/shard_map/ppermute | solution.py:56
  93.2 1.6 collective-permute-done.11.refs_6_
  94.7 0.9 collective-permute-done.13.refs_8_
  95.7 0.8 copy-done.12
  96.6 6.8 %qkv_partial_two.1 = bf16[384,1280]{1,0:T(8,128)(2,1)} custom-call(s32[8]{0:T(128)} %add_multiply_fusion.start_ref, bf16[384,2048]{1,0:T(8,128)(2,1)} %bitcast.18, bf16[256,1280]{1,0:T(8,128)(2,1)} %bitcast.28, bf16[256,1280]{1,0:T(8,128)(2,1)} %collective-permute-done.7.refs_2_, bf16[256,1280]{1,0:T(8,128)(2,1)} %collective-permute-done.4.refs_3_, ...), custom_call_target="tpu_custom_call" | custom-call | flops 2013265920 | bytes 6815744 | tf_op jit(solution)/shard_map/qkv_partial_two/pallas_call | solution.py:309
  103.6 3.7 %collective-permute-start.15 = (bf16[256,2048]{1,0:T(8,128)(2,1)}, bf16[256,2048]{1,0:T(8,128)(2,1)S(1)}, u32[]{:S(2)}, u32[]{:S(2)}) collective-permute-start(bf16[256,2048]{1,0:T(8,128)(2,1)} %bitcast.6.refs_1_), channel_id=1, source_target_pairs={{0,68},{64,0},{4,64},{68,4},{1,69},{65,1},{5,65},{69,5},{2,70},{66... | collective-permute-start | bytes 3145736 | tf_op jit(solution)/shard_map/ppermute | solution.py:56
  107.3 5.9 %all-to-all-start.5 = ((bf16[16,24,1280]{2,1,0:T(8,128)(2,1)}), bf16[16,24,1280]{2,1,0:T(8,128)(2,1)S(1)}, u32[]{:S(2)}, u32[]{:S(2)}) async-start(bf16[16,24,1280]{2,1,0:T(8,128)(2,1)} %bitcast.23), calls=%async_computation.5 | async-start | bytes 1966080 | tf_op jit(solution)/shard_map/all_to_all | solution.py:421
  113.3 7.8 %attention.2.refs_0_ = bf16[16,3,8,2048]{3,2,1,0:T(8,128)(2,1)} custom-call(s32[6]{0:T(128)} %lengths_ref.3, bf16[16,3,8,1280]{3,2,1,0:T(8,128)(2,1)} %bitcast.21, f32[3,8,128]{2,1,0:T(8,128)} %get-tuple-element.64.cos_ref, f32[3,8,128]{2,1,0:T(8,128)} %get-tuple-element.65.sin_ref, bf16[6,512,1024]{2,1,0:T(8,128)(2,1)} %key_ref.3, ...), custom_call_target="tpu_custom_call" | custom-call | flops 402653184 | bytes 6291456 | tf_op jit(solution)/shard_map/attention/pallas_call | solution.py:232
  121.0 9.2 %all-to-all-done.5 = bf16[16,24,1280]{2,1,0:T(8,128)(2,1)S(1)} async-done(((bf16[16,24,1280]{2,1,0:T(8,128)(2,1)}), bf16[16,24,1280]{2,1,0:T(8,128)(2,1)S(1)}, u32[]{:S(2)}, u32[]{:S(2)}) %all-to-all-start.5) | async-done | bytes 983072 | tf_op jit(solution)/shard_map/all_to_all | solution.py:421
  130.7 3.4 %collective-permute-done.14.refs_5_ = bf16[256,2048]{1,0:T(8,128)(2,1)} collective-permute-done((bf16[256,2048]{1,0:T(8,128)(2,1)}, bf16[256,2048]{1,0:T(8,128)(2,1)}, u32[]{:S(2)}, u32[]{:S(2)}) %collective-permute-start.14) | collective-permute-done | bytes 1048608 | tf_op jit(solution)/shard_map/ppermute | solution.py:56
  134.1 0.5 collective-permute-start.20
  134.6 1.1 slice.6
  136.0 1.8 collective-permute-start.17
  137.9 7.7 %attention.3 = bf16[16,3,8,2048]{3,2,1,0:T(8,128)(2,1)} custom-call(s32[6]{0:T(128)} %lengths_ref.3, bf16[16,3,8,1280]{3,2,1,0:T(8,128)(2,1)} %bitcast.24, f32[3,8,128]{2,1,0:T(8,128)} %get-tuple-element.64.cos_ref, f32[3,8,128]{2,1,0:T(8,128)} %get-tuple-element.65.sin_ref, bf16[6,512,1024]{2,1,0:T(8,128)(2,1)} %key_ref.3, ...), custom_call_target="tpu_custom_call", output_to_operand_aliasing={{}: (6, {})} | custom-call | flops 402653184 | bytes 6291456 | tf_op jit(solution)/shard_map/attention/pallas_call | solution.py:232
  145.6 4.1 %collective-permute-done.18.refs_9_ = bf16[128,2048]{1,0:T(8,128)(2,1)S(1)} collective-permute-done((bf16[128,2048]{1,0:T(8,128)(2,1)S(1)}, bf16[128,2048]{1,0:T(8,128)(2,1)S(1)}, u32[]{:S(2)}, u32[]{:S(2)}) %collective-permute-start.18) | collective-permute-done | bytes 524320 | tf_op jit(solution)/shard_map/ppermute | solution.py:56
  149.7 1.3 collective-permute-done.17.refs_7_
  151.0 0.8 copy-done.18
  151.8 5.9 %all-to-all-start.6 = ((bf16[16,3,8,2048]{3,2,1,0:T(8,128)(2,1)}), bf16[16,3,8,2048]{3,2,1,0:T(8,128)(2,1)S(1)}, u32[]{:S(2)}, u32[]{:S(2)}) async-start(bf16[16,3,8,2048]{3,2,1,0:T(8,128)(2,1)} %attention.3), calls=%async_computation.6 | async-start | bytes 3145728 | tf_op jit(solution)/shard_map/all_to_all | solution.py:436
  158.3 1.4 collective-permute-done.21.refs_8_
  159.7 0.9 collective-permute-done.22.refs_10_
  160.6 20.0 %all-to-all-done.6 = bf16[16,3,8,2048]{3,2,1,0:T(8,128)(2,1)S(1)} async-done(((bf16[16,3,8,2048]{3,2,1,0:T(8,128)(2,1)}), bf16[16,3,8,2048]{3,2,1,0:T(8,128)(2,1)S(1)}, u32[]{:S(2)}, u32[]{:S(2)}) %all-to-all-start.6) | async-done | bytes 1572896 | tf_op jit(solution)/shard_map/all_to_all | solution.py:436
  180.6 1.2 copy-done.6
  181.8 9.5 %out_partial.1 = bf16[8,384,256]{2,1,0:T(8,128)(2,1)} custom-call(s32[8]{0:T(128)} %add_multiply_fusion.start_ref, bf16[384,2048]{1,0:T(8,128)(2,1)} %bitcast.33, bf16[256,2048]{1,0:T(8,128)(2,1)} %bitcast.6.refs_1_, bf16[256,2048]{1,0:T(8,128)(2,1)} %collective-permute-done.16.refs_2_, bf16[256,2048]{1,0:T(8,128)(2,1)} %copy-done.14, ...), custom_call_target="tpu_custom_call" | custom-call | flops 3221225472 | bytes 9961472 | tf_op jit(solution)/shard_map/out_partial/pallas_call | solution.py:309
  191.4 23.1 %all_to_all.41 = bf16[8,384,256]{2,1,0:T(8,128)(2,1)S(1)} all-to-all(bf16[8,384,256]{2,1,0:T(8,128)(2,1)} %out_partial.1), channel_id=1, replica_groups=mesh['zl'=2,'c'=2,'y'=4,'zh'=2,'x'=4] {'y','zh'}, dimensions={0} | all-to-all | bytes 3145728 | tf_op jit(solution)/shard_map/all_to_all | solution.py:446
  215.5 0.8 copy.25
  (84 shorter events, 4.7 us)
Async XLA Ops:
  3.3 15.3 %all-to-all-start = ((bf16[4,64,1280]{2,1,0:T(8,128)(2,1)}), bf16[4,64,1280]{2,1,0:T(8,128)(2,1)S(1)}, u32[]{:S(2)}, u32[]{:S(2)}) async-start(bf16[4,64,1280]{2,1,0:T(8,128)(2,1)} %joint_adam.2), calls=%async_computation | async-start | bytes 1310720 | tf_op jit(solution)/shard_map/all_to_all | solution.py:365
  7.7 3.3 %copy-start.15 = (bf16[8192]{0:T(1024)(128)(2,1)S(1)}, bf16[8192]{0:T(1024)(128)(2,1)}, u32[]{:S(2)}) copy-start(bf16[8192]{0:T(1024)(128)(2,1)} %param.14) | copy-start | bytes 49156
  7.7 3.4 %copy-start.13 = (bf16[4,6,8192]{2,0,1:T(4,128)(2,1)S(1)}, bf16[4,6,8192]{2,0,1:T(4,128)(2,1)}, u32[]{:S(2)}) copy-start(bf16[4,6,8192]{2,0,1:T(4,128)(2,1)} %param.13) | copy-start | bytes 1179652
  11.0 11.6 %copy-start.3 = (bf16[4,64,1280]{2,1,0:T(8,128)(2,1)S(1)}, bf16[4,64,1280]{2,1,0:T(8,128)(2,1)}, u32[]{:S(2)}) copy-start(bf16[4,64,1280]{2,1,0:T(8,128)(2,1)} %joint_adam.3) | copy-start | bytes 1966084
  18.6 18.0 %copy-start.5 = (bf16[4,64,1280]{2,1,0:T(8,128)(2,1)}, bf16[4,64,1280]{2,1,0:T(8,128)(2,1)S(1)}, u32[]{:S(2)}) copy-start(bf16[4,64,1280]{2,1,0:T(8,128)(2,1)S(1)} %all-to-all-done) | copy-start | bytes 1966084
  18.6 23.2 %collective-permute-start.2 = (bf16[256,1280]{1,0:T(8,128)(2,1)S(1)}, bf16[256,1280]{1,0:T(8,128)(2,1)}, u32[]{:S(2)}, u32[]{:S(2)}) collective-permute-start(bf16[256,1280]{1,0:T(8,128)(2,1)S(1)} %bitcast.29), channel_id=1, source_target_pairs={{0,32},{32,0},{1,33},{33,1},{2,34},{34,2},{3,35},{35,3},{4,36},{36... | collective-permute-start | bytes 1966088 | tf_op jit(solution)/shard_map/ppermute | solution.py:62
  18.6 23.2 %collective-permute-start.1 = (bf16[256,1280]{1,0:T(8,128)(2,1)S(1)}, bf16[256,1280]{1,0:T(8,128)(2,1)}, u32[]{:S(2)}, u32[]{:S(2)}) collective-permute-start(bf16[256,1280]{1,0:T(8,128)(2,1)S(1)} %bitcast.30), channel_id=1, source_target_pairs={{0,68},{64,0},{4,64},{68,4},{1,69},{65,1},{5,65},{69,5},{2,70},{66... | collective-permute-start | bytes 1966088 | tf_op jit(solution)/shard_map/ppermute | solution.py:56
  22.6 19.2 %collective-permute-start = (bf16[256,1280]{1,0:T(8,128)(2,1)S(1)}, bf16[256,1280]{1,0:T(8,128)(2,1)}, u32[]{:S(2)}, u32[]{:S(2)}) collective-permute-start(bf16[256,1280]{1,0:T(8,128)(2,1)S(1)} %bitcast.31), channel_id=1, source_target_pairs={{0,64},{64,4},{4,68},{68,0},{1,65},{65,5},{5,69},{69,1},{2,66},{66... | collective-permute-start | bytes 1966088 | tf_op jit(solution)/shard_map/ppermute | solution.py:56
  36.6 40.8 %copy-start.4 = (bf16[4,64,1280]{2,1,0:T(8,128)(2,1)}, bf16[4,64,1280]{2,1,0:T(8,128)(2,1)S(1)}, u32[]{:S(2)}) copy-start(bf16[4,64,1280]{2,1,0:T(8,128)(2,1)S(1)} %all_to_all.40) | copy-start | bytes 1966084
  36.6 28.8 %all-to-all-start.2 = ((bf16[16,24,2048]{2,1,0:T(8,128)(2,1)}), bf16[16,24,2048]{2,1,0:T(8,128)(2,1)S(1)}, u32[]{:S(2)}, u32[]{:S(2)}) async-start(bf16[16,24,2048]{2,1,0:T(8,128)(2,1)} %norm_rows.1), calls=%async_computation.2 | async-start | bytes 3145728 | tf_op jit(solution)/shard_map/all_to_all | solution.py:378
  41.8 7.8 %copy-start.16 = (s32[6]{0:T(128)S(1)}, s32[6]{0:T(128)}, u32[]{:S(2)}) copy-start(s32[6]{0:T(128)} %lengths_ref.3) | copy-start | bytes 76
  41.8 12.3 %collective-permute-start.6 = (bf16[256,1280]{1,0:T(8,128)(2,1)}, bf16[256,1280]{1,0:T(8,128)(2,1)}, u32[]{:S(2)}, u32[]{:S(2)}) collective-permute-start(bf16[256,1280]{1,0:T(8,128)(2,1)} %collective-permute-done.refs_5_), channel_id=1, source_target_pairs={{0,32},{32,0},{1,33},{33,1},{2,34},{34,2},{3,35},{35,3},{4,36},{36... | collective-permute-start | bytes 1966088 | tf_op jit(solution)/shard_map/ppermute | solution.py:62
  41.9 18.7 %collective-permute-start.3 = (bf16[256,1280]{1,0:T(8,128)(2,1)}, bf16[256,1280]{1,0:T(8,128)(2,1)}, u32[]{:S(2)}, u32[]{:S(2)}) collective-permute-start(bf16[256,1280]{1,0:T(8,128)(2,1)} %collective-permute-done.refs_5_), channel_id=1, source_target_pairs={{0,64},{64,4},{4,68},{68,0},{1,65},{65,5},{5,69},{69,1},{2,66},{66... | collective-permute-start | bytes 1966088 | tf_op jit(solution)/shard_map/ppermute | solution.py:56
  42.0 18.6 %collective-permute-start.7 = (bf16[256,1280]{1,0:T(8,128)(2,1)S(1)}, bf16[256,1280]{1,0:T(8,128)(2,1)}, u32[]{:S(2)}, u32[]{:S(2)}) collective-permute-start(bf16[256,1280]{1,0:T(8,128)(2,1)S(1)} %bitcast.25), channel_id=1, source_target_pairs={{0,32},{32,0},{1,33},{33,1},{2,34},{34,2},{3,35},{35,3},{4,36},{36... | collective-permute-start | bytes 1966088 | tf_op jit(solution)/shard_map/ppermute | solution.py:62
  42.4 18.2 %collective-permute-start.4 = (bf16[256,1280]{1,0:T(8,128)(2,1)S(1)}, bf16[256,1280]{1,0:T(8,128)(2,1)}, u32[]{:S(2)}, u32[]{:S(2)}) collective-permute-start(bf16[256,1280]{1,0:T(8,128)(2,1)S(1)} %bitcast.26), channel_id=1, source_target_pairs={{0,68},{64,0},{4,64},{68,4},{1,69},{65,1},{5,65},{69,5},{2,70},{66... | collective-permute-start | bytes 1966088 | tf_op jit(solution)/shard_map/ppermute | solution.py:56
  45.4 8.7 %collective-permute-start.5 = (bf16[256,1280]{1,0:T(8,128)(2,1)}, bf16[256,1280]{1,0:T(8,128)(2,1)}, u32[]{:S(2)}, u32[]{:S(2)}) collective-permute-start(bf16[256,1280]{1,0:T(8,128)(2,1)} %collective-permute-done.1.refs_3_), channel_id=1, source_target_pairs={{0,32},{32,0},{1,33},{33,1},{2,34},{34,2},{3,35},{35,3},{4,36},{36... | collective-permute-start | bytes 1966088 | tf_op jit(solution)/shard_map/ppermute | solution.py:62
  60.6 9.1 %collective-permute-start.8 = (bf16[256,1280]{1,0:T(8,128)(2,1)}, bf16[256,1280]{1,0:T(8,128)(2,1)S(1)}, u32[]{:S(2)}, u32[]{:S(2)}) collective-permute-start(bf16[256,1280]{1,0:T(8,128)(2,1)} %collective-permute-done.3.refs_7_), channel_id=1, source_target_pairs={{0,32},{32,0},{1,33},{33,1},{2,34},{34,2},{3,35},{35,3},{4,36},{36... | collective-permute-start | bytes 1966088 | tf_op jit(solution)/shard_map/ppermute | solution.py:62
  65.4 4.3 %copy-start = (bf16[16,24,2048]{2,1,0:T(8,128)(2,1)}, bf16[16,24,2048]{2,1,0:T(8,128)(2,1)S(1)}, u32[]{:S(2)}) copy-start(bf16[16,24,2048]{2,1,0:T(8,128)(2,1)S(1)} %all-to-all-done.2) | copy-start | bytes 4718596
  65.4 17.1 %all-to-all-start.4 = ((bf16[4,64,2048]{2,1,0:T(8,128)(2,1)}), bf16[4,64,2048]{2,1,0:T(8,128)(2,1)}, u32[]{:S(2)}, u32[]{:S(2)}) async-start(bf16[4,64,2048]{2,1,0:T(8,128)(2,1)} %reshape.87), calls=%async_computation.4 | async-start | bytes 2097152 | tf_op jit(solution)/shard_map/all_to_all | solution.py:365
  77.3 15.3 %collective-permute-start.10 = (bf16[256,1280]{1,0:T(8,128)(2,1)S(1)}, bf16[256,1280]{1,0:T(8,128)(2,1)S(1)}, u32[]{:S(2)}, u32[]{:S(2)}) collective-permute-start(bf16[256,1280]{1,0:T(8,128)(2,1)S(1)} %bitcast.27), channel_id=1, source_target_pairs={{0,64},{64,4},{4,68},{68,0},{1,65},{65,5},{5,69},{69,1},{2,66},{66... | collective-permute-start | bytes 1966088 | tf_op jit(solution)/shard_map/ppermute | solution.py:56
  77.4 15.2 %collective-permute-start.12 = (bf16[256,1280]{1,0:T(8,128)(2,1)}, bf16[256,1280]{1,0:T(8,128)(2,1)S(1)}, u32[]{:S(2)}, u32[]{:S(2)}) collective-permute-start(bf16[256,1280]{1,0:T(8,128)(2,1)} %collective-permute-done.4.refs_3_), channel_id=1, source_target_pairs={{0,68},{64,0},{4,64},{68,4},{1,69},{65,1},{5,65},{69,5},{2,70},{66... | collective-permute-start | bytes 1966088 | tf_op jit(solution)/shard_map/ppermute | solution.py:56
  82.5 20.9 %all-to-all-start.3 = ((bf16[16,24,1280]{2,1,0:T(8,128)(2,1)}), bf16[16,24,1280]{2,1,0:T(8,128)(2,1)S(1)}, u32[]{:S(2)}, u32[]{:S(2)}) async-start(bf16[16,24,1280]{2,1,0:T(8,128)(2,1)} %bitcast.22), calls=%async_computation.3 | async-start | bytes 1966080 | tf_op jit(solution)/shard_map/all_to_all | solution.py:409
  87.8 5.4 %collective-permute-start.9 = (bf16[256,1280]{1,0:T(8,128)(2,1)}, bf16[256,1280]{1,0:T(8,128)(2,1)S(1)}, u32[]{:S(2)}, u32[]{:S(2)}) collective-permute-start(bf16[256,1280]{1,0:T(8,128)(2,1)} %collective-permute-done.4.refs_3_), channel_id=1, source_target_pairs={{0,32},{32,0},{1,33},{33,1},{2,34},{34,2},{3,35},{35,3},{4,36},{36... | collective-permute-start | bytes 1966088 | tf_op jit(solution)/shard_map/ppermute | solution.py:62
  92.6 3.0 %copy-start.7 = (bf16[256,1280]{1,0:T(8,128)(2,1)}, bf16[256,1280]{1,0:T(8,128)(2,1)S(1)}, u32[]{:S(2)}) copy-start(bf16[256,1280]{1,0:T(8,128)(2,1)S(1)} %collective-permute-done.10.refs_5_) | copy-start | bytes 1966084
  92.6 2.1 collective-permute-start.11
  92.6 3.0 %copy-start.8 = (bf16[256,1280]{1,0:T(8,128)(2,1)}, bf16[256,1280]{1,0:T(8,128)(2,1)S(1)}, u32[]{:S(2)}) copy-start(bf16[256,1280]{1,0:T(8,128)(2,1)S(1)} %collective-permute-done.12.refs_7_) | copy-start | bytes 1966084
  92.7 3.0 %collective-permute-start.13 = (bf16[256,1280]{1,0:T(8,128)(2,1)S(1)}, bf16[256,1280]{1,0:T(8,128)(2,1)S(1)}, u32[]{:S(2)}, u32[]{:S(2)}) collective-permute-start(bf16[256,1280]{1,0:T(8,128)(2,1)S(1)} %collective-permute-done.12.refs_7_), channel_id=1, source_target_pairs={{0,32},{32,0},{1,33},{33,1},{2,34},{34,2},{3,35},{35,3},{4,36},{36... | collective-permute-start | bytes 1966088 | tf_op jit(solution)/shard_map/ppermute | solution.py:62
  93.2 2.5 %copy-start.10 = (bf16[256,1280]{1,0:T(8,128)(2,1)}, bf16[256,1280]{1,0:T(8,128)(2,1)S(1)}, u32[]{:S(2)}) copy-start(bf16[256,1280]{1,0:T(8,128)(2,1)S(1)} %collective-permute-done.9.refs_4_) | copy-start | bytes 1966084
  94.7 0.9 copy-start.11
  95.7 0.9 copy-start.12
  103.4 9.8 %copy-start.1 = (bf16[16,24,1280]{2,1,0:T(8,128)(2,1)}, bf16[16,24,1280]{2,1,0:T(8,128)(2,1)S(1)}, u32[]{:S(2)}) copy-start(bf16[16,24,1280]{2,1,0:T(8,128)(2,1)S(1)} %all-to-all-done.3) | copy-start | bytes 2949124
  103.4 26.8 %collective-permute-start.16 = (bf16[256,2048]{1,0:T(8,128)(2,1)}, bf16[256,2048]{1,0:T(8,128)(2,1)}, u32[]{:S(2)}, u32[]{:S(2)}) collective-permute-start(bf16[256,2048]{1,0:T(8,128)(2,1)} %bitcast.6.refs_1_), channel_id=1, source_target_pairs={{0,32},{32,0},{1,33},{33,1},{2,34},{34,2},{3,35},{35,3},{4,36},{36... | collective-permute-start | bytes 3145736 | tf_op jit(solution)/shard_map/ppermute | solution.py:62
  103.6 27.1 %collective-permute-start.15 = (bf16[256,2048]{1,0:T(8,128)(2,1)}, bf16[256,2048]{1,0:T(8,128)(2,1)S(1)}, u32[]{:S(2)}, u32[]{:S(2)}) collective-permute-start(bf16[256,2048]{1,0:T(8,128)(2,1)} %bitcast.6.refs_1_), channel_id=1, source_target_pairs={{0,68},{64,0},{4,64},{68,4},{1,69},{65,1},{5,65},{69,5},{2,70},{66... | collective-permute-start | bytes 3145736 | tf_op jit(solution)/shard_map/ppermute | solution.py:56
  107.3 26.8 %collective-permute-start.14 = (bf16[256,2048]{1,0:T(8,128)(2,1)}, bf16[256,2048]{1,0:T(8,128)(2,1)}, u32[]{:S(2)}, u32[]{:S(2)}) collective-permute-start(bf16[256,2048]{1,0:T(8,128)(2,1)} %bitcast.6.refs_1_), channel_id=1, source_target_pairs={{0,64},{64,4},{4,68},{68,0},{1,65},{65,5},{5,69},{69,1},{2,66},{66... | collective-permute-start | bytes 3145736 | tf_op jit(solution)/shard_map/ppermute | solution.py:56
  107.3 22.9 %all-to-all-start.5 = ((bf16[16,24,1280]{2,1,0:T(8,128)(2,1)}), bf16[16,24,1280]{2,1,0:T(8,128)(2,1)S(1)}, u32[]{:S(2)}, u32[]{:S(2)}) async-start(bf16[16,24,1280]{2,1,0:T(8,128)(2,1)} %bitcast.23), calls=%async_computation.5 | async-start | bytes 1966080 | tf_op jit(solution)/shard_map/all_to_all | solution.py:421
  130.2 7.6 %copy-start.2 = (bf16[16,24,1280]{2,1,0:T(8,128)(2,1)}, bf16[16,24,1280]{2,1,0:T(8,128)(2,1)S(1)}, u32[]{:S(2)}) copy-start(bf16[16,24,1280]{2,1,0:T(8,128)(2,1)S(1)} %all-to-all-done.5) | copy-start | bytes 2949124
  130.7 14.9 %copy-start.14 = (bf16[256,2048]{1,0:T(8,128)(2,1)}, bf16[256,2048]{1,0:T(8,128)(2,1)S(1)}, u32[]{:S(2)}) copy-start(bf16[256,2048]{1,0:T(8,128)(2,1)S(1)} %collective-permute-done.15.refs_3_) | copy-start | bytes 3145732
  134.1 17.7 %collective-permute-start.19 = (bf16[256,2048]{1,0:T(8,128)(2,1)}, bf16[256,2048]{1,0:T(8,128)(2,1)}, u32[]{:S(2)}, u32[]{:S(2)}) collective-permute-start(bf16[256,2048]{1,0:T(8,128)(2,1)} %collective-permute-done.14.refs_5_), channel_id=1, source_target_pairs={{0,32},{32,0},{1,33},{33,1},{2,34},{34,2},{3,35},{35,3},{4,36},{36... | collective-permute-start | bytes 3145736 | tf_op jit(solution)/shard_map/ppermute | solution.py:62
  134.1 17.7 %collective-permute-start.20 = (bf16[256,2048]{1,0:T(8,128)(2,1)S(1)}, bf16[256,2048]{1,0:T(8,128)(2,1)}, u32[]{:S(2)}, u32[]{:S(2)}) collective-permute-start(bf16[256,2048]{1,0:T(8,128)(2,1)S(1)} %collective-permute-done.15.refs_3_), channel_id=1, source_target_pairs={{0,32},{32,0},{1,33},{33,1},{2,34},{34,2},{3,35},{35,3},{4,36},{36... | collective-permute-start | bytes 3145736 | tf_op jit(solution)/shard_map/ppermute | solution.py:62
  135.8 13.9 %collective-permute-start.18 = (bf16[128,2048]{1,0:T(8,128)(2,1)S(1)}, bf16[128,2048]{1,0:T(8,128)(2,1)S(1)}, u32[]{:S(2)}, u32[]{:S(2)}) collective-permute-start(bf16[128,2048]{1,0:T(8,128)(2,1)S(1)} %slice.7), channel_id=1, source_target_pairs={{0,68},{64,0},{4,64},{68,4},{1,69},{65,1},{5,65},{69,5},{2,70},{66... | collective-permute-start | bytes 1572872 | tf_op jit(solution)/shard_map/ppermute | solution.py:56
  136.0 14.9 %collective-permute-start.17 = (bf16[128,2048]{1,0:T(8,128)(2,1)S(1)}, bf16[128,2048]{1,0:T(8,128)(2,1)S(1)}, u32[]{:S(2)}, u32[]{:S(2)}) collective-permute-start(bf16[128,2048]{1,0:T(8,128)(2,1)S(1)} %slice.6), channel_id=1, source_target_pairs={{0,64},{64,4},{4,68},{68,0},{1,65},{65,5},{5,69},{69,1},{2,66},{66... | collective-permute-start | bytes 1572872 | tf_op jit(solution)/shard_map/ppermute | solution.py:56
  149.7 30.9 %copy-start.17 = (bf16[128,2048]{1,0:T(8,128)(2,1)}, bf16[128,2048]{1,0:T(8,128)(2,1)S(1)}, u32[]{:S(2)}) copy-start(bf16[128,2048]{1,0:T(8,128)(2,1)S(1)} %collective-permute-done.18.refs_9_) | copy-start | bytes 1572868
  151.8 5.9 %copy-start.19 = (bf16[128,2048]{1,0:T(8,128)(2,1)S(1)}, bf16[128,2048]{1,0:T(8,128)(2,1)}, u32[]{:S(2)}) copy-start(bf16[128,2048]{1,0:T(8,128)(2,1)} %copy-done.18) | copy-start | bytes 1572868
  151.8 28.8 %all-to-all-start.6 = ((bf16[16,3,8,2048]{3,2,1,0:T(8,128)(2,1)}), bf16[16,3,8,2048]{3,2,1,0:T(8,128)(2,1)S(1)}, u32[]{:S(2)}, u32[]{:S(2)}) async-start(bf16[16,3,8,2048]{3,2,1,0:T(8,128)(2,1)} %attention.3), calls=%async_computation.6 | async-start | bytes 3145728 | tf_op jit(solution)/shard_map/all_to_all | solution.py:436
  157.7 2.0 collective-permute-start.21
  157.8 2.8 %collective-permute-start.22 = (bf16[128,2048]{1,0:T(8,128)(2,1)S(1)}, bf16[128,2048]{1,0:T(8,128)(2,1)}, u32[]{:S(2)}, u32[]{:S(2)}) collective-permute-start(bf16[128,2048]{1,0:T(8,128)(2,1)S(1)} %collective-permute-done.18.refs_9_), channel_id=1, source_target_pairs={{0,32},{32,0},{1,33},{33,1},{2,34},{34,2},{3,35},{35,3},{4,36},{36... | collective-permute-start | bytes 1572872 | tf_op jit(solution)/shard_map/ppermute | solution.py:62
  159.7 20.9 %copy-start.20 = (bf16[128,2048]{1,0:T(8,128)(2,1)}, bf16[128,2048]{1,0:T(8,128)(2,1)S(1)}, u32[]{:S(2)}) copy-start(bf16[128,2048]{1,0:T(8,128)(2,1)S(1)} %collective-permute-done.21.refs_8_) | copy-start | bytes 1572868
  180.6 1.2 copy-start.6
  (2 other events, 1.7 us)

commit v3 on v2

--- a/solution.py
+++ b/solution.py
@@ -430,9 +430,6 @@
     out_far = shift_z(out_below[:half], 1), shift_z(out_above[half:], -1)
     out_below_swapped, out_above_swapped = swap_cores(out_below), swap_cores(out_above)
     attended = attention(1, fields_two.reshape(fields_shape), cosine, sine, *caches, attended)
-    attended, out_far, out_below_swapped, out_above_swapped = barrier(
-        (attended, out_far, out_below_swapped, out_above_swapped)
-    )
     attended = lax.all_to_all(attended, PLANE, split_axis=0, concat_axis=0, tiled=True)
     pieces = both_cores(
         (0, 0, out_own, out_own_swapped),

time: 218 us -> 209 us (0.959)
  waiting for transfers between devices: 65.3 us -> 53.7 us
    all_to_all x1, waiting for transfers between devices: 20 us -> 3.69 us  [body(): lax.all_to_all(attended, PLANE, split_axis=0, concat_axis=0, tiled=True)]
    ppermute x10, waiting for transfers between devices: 20.5 us -> 25.4 us  [shift_z(): lax.ppermute(value, ('zl', 'zh'), [(position(z), position(z + step + Z_SI...]
    unnamed x43 -> x45, local copies, waits for them, and re-layouts: 4.03 us -> 5 us
  transfers between devices with their start and end apart: 29 -> 29, of which waited for: 15 -> 14; matrix products, arithmetic and copies ran while one was open for 5% -> 5% of each run, Pallas kernels for 16% -> 13%
where the time goes in v3:
time: 209 us; the launch traced here: 207 us
  waiting for transfers between devices  53.7 us (26%)
  starting transfers between devices  50.5 us (24%)
  Pallas kernels  47.3 us (23%)
  blocking collectives  37.7 us (18%)
  local copies, waits for them, and re-layouts  12 us (6%)
  other arithmetic  5.89 us (3%)
    ppermute x10, waiting for transfers between devices, shift_z(): lax.ppermute(value, ('zl', 'zh'), [(position(z), position(z + step + Z_SI...  25.4 us
    all_to_all x1, blocking collectives, body(): lax.all_to_all(partial, ('y', 'zh'), split_axis=0, concat_axis=0, tiled=T...  23.8 us
    pallas_call x3, Pallas kernels, product(): pl.pallas_call(functools.partial(product_kernel, len(rows), places, by_bl...  23.2 us
    ppermute x10, starting transfers between devices, shift_z(): lax.ppermute(value, ('zl', 'zh'), [(position(z), position(z + step + Z_SI...  17.5 us
    pallas_call x2, Pallas kernels, attention(): pl.pallas_call(attention_kernel, out_shape=jax.ShapeDtypeStruct((16, PAIR...  15.5 us
    all_to_all x1, blocking collectives, to_owner(): piece = lax.all_to_all(piece, 'x', split_axis=0, concat_axis=0, tiled=True)  13.9 us
    all_to_all x1, waiting for transfers between devices, body(): lax.all_to_all(projected_two, PLANE, split_axis=0, concat_axis=0, tiled=T...  9.25 us
    all_to_all x2, starting transfers between devices, to_owner(): piece = lax.all_to_all(piece, 'x', split_axis=0, concat_axis=0, tiled=True)  8.62 us
  transfers between devices with their start and end apart: 29, of which 14 were waited for; matrix products, arithmetic and copies ran while one was open for 5% of the time, Pallas kernels for 13%

profile of v3, /device:TPU:0, one launch (start us, length us, event | category | flops | bytes accessed | tf_op | source)
XLA Modules:
  0.0 207.5 jit_solution(17777279225989427462)
XLA Ops:
  0.0 3.3 %joint_adam.2 = bf16[4,64,1280]{2,1,0:T(8,128)(2,1)} custom-call(bf16[64,10240]{1,0:T(8,128)(2,1)} %refs_2_.3, bf16[64,10240]{1,0:T(8,128)(2,1)} %refs_2_.3, bf16[64,10240]{1,0:T(8,128)(2,1)} %refs_2_.3, bf16[64,10240]{1,0:T(8,128)(2,1)} %refs_5_.3, bf16[64,10240]{1,0:T(8,128)(2,1)} %refs_5_.3, bf16[64,10240]{1,0:T(8,128)(2,1)} %refs_5_.3, ...), custom_call_target="tpu_custom_call" | custom-call | tf_op jit(solution)/shard_map/joint_adam/pallas_call | solution.py:83
  3.3 4.4 %all-to-all-start = ((bf16[4,64,1280]{2,1,0:T(8,128)(2,1)}), bf16[4,64,1280]{2,1,0:T(8,128)(2,1)S(1)}, u32[]{:S(2)}, u32[]{:S(2)}) async-start(bf16[4,64,1280]{2,1,0:T(8,128)(2,1)} %joint_adam.2), calls=%async_computation | async-start | bytes 1310720 | tf_op jit(solution)/shard_map/all_to_all | solution.py:365
  7.7 3.3 %joint_adam.3 = bf16[4,64,1280]{2,1,0:T(8,128)(2,1)} custom-call(bf16[64,10240]{1,0:T(8,128)(2,1)} %refs_2_.3, bf16[64,10240]{1,0:T(8,128)(2,1)} %refs_2_.3, bf16[64,10240]{1,0:T(8,128)(2,1)} %refs_2_.3, bf16[64,10240]{1,0:T(8,128)(2,1)} %refs_5_.3, bf16[64,10240]{1,0:T(8,128)(2,1)} %refs_5_.3, bf16[64,10240]{1,0:T(8,128)(2,1)} %refs_5_.3, ...), custom_call_target="tpu_custom_call" | custom-call | tf_op jit(solution)/shard_map/joint_adam/pallas_call | solution.py:83
  11.3 1.9 norm_rows.1
  13.2 5.4 %all-to-all-done = bf16[4,64,1280]{2,1,0:T(8,128)(2,1)S(1)} async-done(((bf16[4,64,1280]{2,1,0:T(8,128)(2,1)}), bf16[4,64,1280]{2,1,0:T(8,128)(2,1)S(1)}, u32[]{:S(2)}, u32[]{:S(2)}) %all-to-all-start) | async-done | bytes 655392 | tf_op jit(solution)/shard_map/all_to_all | solution.py:365
  18.6 4.0 %collective-permute-start.1 = (bf16[256,1280]{1,0:T(8,128)(2,1)S(1)}, bf16[256,1280]{1,0:T(8,128)(2,1)}, u32[]{:S(2)}, u32[]{:S(2)}) collective-permute-start(bf16[256,1280]{1,0:T(8,128)(2,1)S(1)} %bitcast.30), channel_id=1, source_target_pairs={{0,68},{64,0},{4,64},{68,4},{1,69},{65,1},{5,65},{69,5},{2,70},{66... | collective-permute-start | bytes 1966088 | tf_op jit(solution)/shard_map/ppermute | solution.py:56
  22.6 13.9 %all_to_all.40 = bf16[4,64,1280]{2,1,0:T(8,128)(2,1)S(1)} all-to-all(bf16[4,64,1280]{2,1,0:T(8,128)(2,1)S(1)} %copy-done.3), channel_id=1, replica_groups=mesh['zl'=2,'c'=2,'y'=4,'zh'=2,'x'=4] {'x'}, dimensions={0} | all-to-all | bytes 1310720 | tf_op jit(solution)/shard_map/all_to_all | solution.py:365
  36.6 5.2 %all-to-all-start.2 = ((bf16[16,24,2048]{2,1,0:T(8,128)(2,1)}), bf16[16,24,2048]{2,1,0:T(8,128)(2,1)S(1)}, u32[]{:S(2)}, u32[]{:S(2)}) async-start(bf16[16,24,2048]{2,1,0:T(8,128)(2,1)} %norm_rows.1), calls=%async_computation.2 | async-start | bytes 3145728 | tf_op jit(solution)/shard_map/all_to_all | solution.py:378
  42.4 3.0 %collective-permute-start.4 = (bf16[256,1280]{1,0:T(8,128)(2,1)S(1)}, bf16[256,1280]{1,0:T(8,128)(2,1)}, u32[]{:S(2)}, u32[]{:S(2)}) collective-permute-start(bf16[256,1280]{1,0:T(8,128)(2,1)S(1)} %bitcast.26), channel_id=1, source_target_pairs={{0,68},{64,0},{4,64},{68,4},{1,69},{65,1},{5,65},{69,5},{2,70},{66... | collective-permute-start | bytes 1966088 | tf_op jit(solution)/shard_map/ppermute | solution.py:56
  45.5 4.0 %fusion.2 = bf16[64,8192]{1,0:T(8,128)(2,1)S(1)} fusion(bf16[64,8192]{1,0:T(8,128)(2,1)} %param.22, bf16[64,8192]{1,0:T(8,128)(2,1)} %param.23, bf16[64,8192]{1,0:T(8,128)(2,1)} %param.25, bf16[64,8192]{1,0:T(8,128)(2,1)} %param.24), kind=kLoop, calls=%fused_computation.6 | loop fusion | flops 10485760 | bytes 5242880 | tf_op jit(solution)/shard_map/convert_element_type | solution.py:43
  49.8 1.6 reshape.86
  51.4 1.4 copy.22
  52.8 1.3 reshape.87
  54.1 6.5 %collective-permute-done.3.refs_7_ = bf16[256,1280]{1,0:T(8,128)(2,1)} collective-permute-done((bf16[256,1280]{1,0:T(8,128)(2,1)}, bf16[256,1280]{1,0:T(8,128)(2,1)}, u32[]{:S(2)}, u32[]{:S(2)}) %collective-permute-start.3) | collective-permute-done | bytes 655392 | tf_op jit(solution)/shard_map/ppermute | solution.py:56
  60.6 0.6 add_multiply_fusion.start_ref
  61.3 0.7 pad_maximum_fusion
  62.0 3.4 %all-to-all-done.2 = bf16[16,24,2048]{2,1,0:T(8,128)(2,1)S(1)} async-done(((bf16[16,24,2048]{2,1,0:T(8,128)(2,1)}), bf16[16,24,2048]{2,1,0:T(8,128)(2,1)S(1)}, u32[]{:S(2)}, u32[]{:S(2)}) %all-to-all-start.2) | async-done | bytes 1572896 | tf_op jit(solution)/shard_map/all_to_all | solution.py:378
  65.4 4.2 %all-to-all-start.4 = ((bf16[4,64,2048]{2,1,0:T(8,128)(2,1)}), bf16[4,64,2048]{2,1,0:T(8,128)(2,1)}, u32[]{:S(2)}, u32[]{:S(2)}) async-start(bf16[4,64,2048]{2,1,0:T(8,128)(2,1)} %reshape.87), calls=%async_computation.4 | async-start | bytes 2097152 | tf_op jit(solution)/shard_map/all_to_all | solution.py:365
  69.7 0.8 copy-done.9
  70.5 6.8 %qkv_partial_one.1 = bf16[384,1280]{1,0:T(8,128)(2,1)} custom-call(s32[8]{0:T(128)} %add_multiply_fusion.start_ref, bf16[384,2048]{1,0:T(8,128)(2,1)} %bitcast.17, bf16[256,1280]{1,0:T(8,128)(2,1)} %bitcast.32, bf16[256,1280]{1,0:T(8,128)(2,1)} %collective-permute-done.2.refs_2_, bf16[256,1280]{1,0:T(8,128)(2,1)} %collective-permute-done.1.refs_3_, ...), custom_call_target="tpu_custom_call" | custom-call | flops 2013265920 | bytes 6815744 | tf_op jit(solution)/shard_map/qkv_partial_one/pallas_call | solution.py:309
  77.4 3.2 %collective-permute-start.12 = (bf16[256,1280]{1,0:T(8,128)(2,1)}, bf16[256,1280]{1,0:T(8,128)(2,1)S(1)}, u32[]{:S(2)}, u32[]{:S(2)}) collective-permute-start(bf16[256,1280]{1,0:T(8,128)(2,1)} %collective-permute-done.4.refs_3_), channel_id=1, source_target_pairs={{0,68},{64,0},{4,64},{68,4},{1,69},{65,1},{5,65},{69,5},{2,70},{66... | collective-permute-start | bytes 1966088 | tf_op jit(solution)/shard_map/ppermute | solution.py:56
  80.7 1.9 all-to-all-done.4
  82.6 5.2 %all-to-all-start.3 = ((bf16[16,24,1280]{2,1,0:T(8,128)(2,1)}), bf16[16,24,1280]{2,1,0:T(8,128)(2,1)S(1)}, u32[]{:S(2)}, u32[]{:S(2)}) async-start(bf16[16,24,1280]{2,1,0:T(8,128)(2,1)} %bitcast.22), calls=%async_computation.3 | async-start | bytes 1966080 | tf_op jit(solution)/shard_map/all_to_all | solution.py:409
  87.9 4.8 %collective-permute-done.10.refs_5_ = bf16[256,1280]{1,0:T(8,128)(2,1)S(1)} collective-permute-done((bf16[256,1280]{1,0:T(8,128)(2,1)S(1)}, bf16[256,1280]{1,0:T(8,128)(2,1)S(1)}, u32[]{:S(2)}, u32[]{:S(2)}) %collective-permute-start.10) | collective-permute-done | bytes 655392 | tf_op jit(solution)/shard_map/ppermute | solution.py:56
  93.2 1.6 collective-permute-done.11.refs_6_
  94.8 0.9 collective-permute-done.13.refs_8_
  95.8 0.8 copy-done.12
  96.6 6.8 %qkv_partial_two.1 = bf16[384,1280]{1,0:T(8,128)(2,1)} custom-call(s32[8]{0:T(128)} %add_multiply_fusion.start_ref, bf16[384,2048]{1,0:T(8,128)(2,1)} %bitcast.18, bf16[256,1280]{1,0:T(8,128)(2,1)} %bitcast.28, bf16[256,1280]{1,0:T(8,128)(2,1)} %collective-permute-done.7.refs_2_, bf16[256,1280]{1,0:T(8,128)(2,1)} %collective-permute-done.4.refs_3_, ...), custom_call_target="tpu_custom_call" | custom-call | flops 2013265920 | bytes 6815744 | tf_op jit(solution)/shard_map/qkv_partial_two/pallas_call | solution.py:309
  103.7 3.7 %collective-permute-start.15 = (bf16[256,2048]{1,0:T(8,128)(2,1)}, bf16[256,2048]{1,0:T(8,128)(2,1)S(1)}, u32[]{:S(2)}, u32[]{:S(2)}) collective-permute-start(bf16[256,2048]{1,0:T(8,128)(2,1)} %bitcast.6.refs_1_), channel_id=1, source_target_pairs={{0,68},{64,0},{4,64},{68,4},{1,69},{65,1},{5,65},{69,5},{2,70},{66... | collective-permute-start | bytes 3145736 | tf_op jit(solution)/shard_map/ppermute | solution.py:56
  107.4 5.9 %all-to-all-start.5 = ((bf16[16,24,1280]{2,1,0:T(8,128)(2,1)}), bf16[16,24,1280]{2,1,0:T(8,128)(2,1)S(1)}, u32[]{:S(2)}, u32[]{:S(2)}) async-start(bf16[16,24,1280]{2,1,0:T(8,128)(2,1)} %bitcast.23), calls=%async_computation.5 | async-start | bytes 1966080 | tf_op jit(solution)/shard_map/all_to_all | solution.py:421
  113.3 7.7 %attention.2.refs_0_ = bf16[16,3,8,2048]{3,2,1,0:T(8,128)(2,1)} custom-call(s32[6]{0:T(128)} %lengths_ref.3, bf16[16,3,8,1280]{3,2,1,0:T(8,128)(2,1)} %bitcast.21, f32[3,8,128]{2,1,0:T(8,128)} %get-tuple-element.59.cos_ref, f32[3,8,128]{2,1,0:T(8,128)} %get-tuple-element.60.sin_ref, bf16[6,512,1024]{2,1,0:T(8,128)(2,1)} %key_ref.3, ...), custom_call_target="tpu_custom_call" | custom-call | flops 402653184 | bytes 6291456 | tf_op jit(solution)/shard_map/attention/pallas_call | solution.py:232
  121.0 9.2 %all-to-all-done.5 = bf16[16,24,1280]{2,1,0:T(8,128)(2,1)S(1)} async-done(((bf16[16,24,1280]{2,1,0:T(8,128)(2,1)}), bf16[16,24,1280]{2,1,0:T(8,128)(2,1)S(1)}, u32[]{:S(2)}, u32[]{:S(2)}) %all-to-all-start.5) | async-done | bytes 983072 | tf_op jit(solution)/shard_map/all_to_all | solution.py:421
  130.8 3.4 %collective-permute-done.14.refs_5_ = bf16[256,2048]{1,0:T(8,128)(2,1)} collective-permute-done((bf16[256,2048]{1,0:T(8,128)(2,1)}, bf16[256,2048]{1,0:T(8,128)(2,1)}, u32[]{:S(2)}, u32[]{:S(2)}) %collective-permute-start.14) | collective-permute-done | bytes 1048608 | tf_op jit(solution)/shard_map/ppermute | solution.py:56
  134.2 7.8 %attention.3 = bf16[16,3,8,2048]{3,2,1,0:T(8,128)(2,1)} custom-call(s32[6]{0:T(128)} %lengths_ref.3, bf16[16,3,8,1280]{3,2,1,0:T(8,128)(2,1)} %bitcast.24, f32[3,8,128]{2,1,0:T(8,128)} %get-tuple-element.59.cos_ref, f32[3,8,128]{2,1,0:T(8,128)} %get-tuple-element.60.sin_ref, bf16[6,512,1024]{2,1,0:T(8,128)(2,1)} %key_ref.3, ...), custom_call_target="tpu_custom_call", output_to_operand_aliasing={{}: (6, {})} | custom-call | flops 402653184 | bytes 6291456 | tf_op jit(solution)/shard_map/attention/pallas_call | solution.py:232
  142.0 5.8 %all-to-all-start.6 = ((bf16[16,3,8,2048]{3,2,1,0:T(8,128)(2,1)}), bf16[16,3,8,2048]{3,2,1,0:T(8,128)(2,1)S(1)}, u32[]{:S(2)}, u32[]{:S(2)}) async-start(bf16[16,3,8,2048]{3,2,1,0:T(8,128)(2,1)} %attention.3), calls=%async_computation.6 | async-start | bytes 3145728 | tf_op jit(solution)/shard_map/all_to_all | solution.py:433
  147.8 1.1 slice.6
  149.0 3.3 %collective-permute-start.21 = (bf16[128,2048]{1,0:T(8,128)(2,1)S(1)}, bf16[128,2048]{1,0:T(8,128)(2,1)S(1)}, u32[]{:S(2)}, u32[]{:S(2)}) collective-permute-start(bf16[128,2048]{1,0:T(8,128)(2,1)S(1)} %slice.7), channel_id=1, source_target_pairs={{0,68},{64,0},{4,64},{68,4},{1,69},{65,1},{5,65},{69,5},{2,70},{66... | collective-permute-start | bytes 1572872 | tf_op jit(solution)/shard_map/ppermute | solution.py:56
  152.3 0.5 collective-permute-start.18
  152.8 10.1 %collective-permute-done.19.refs_7_ = bf16[128,2048]{1,0:T(8,128)(2,1)S(1)} collective-permute-done((bf16[128,2048]{1,0:T(8,128)(2,1)S(1)}, bf16[128,2048]{1,0:T(8,128)(2,1)S(1)}, u32[]{:S(2)}, u32[]{:S(2)}) %collective-permute-start.19) | collective-permute-done | bytes 524320 | tf_op jit(solution)/shard_map/ppermute | solution.py:56
  163.4 1.4 collective-permute-done.20.refs_8_
  164.8 0.7 collective-permute-done.22.refs_10_
  165.6 0.8 copy-done.21
  166.4 1.0 copy-done.17
  167.4 3.7 %all-to-all-done.6 = bf16[16,3,8,2048]{3,2,1,0:T(8,128)(2,1)S(1)} async-done(((bf16[16,3,8,2048]{3,2,1,0:T(8,128)(2,1)}), bf16[16,3,8,2048]{3,2,1,0:T(8,128)(2,1)S(1)}, u32[]{:S(2)}, u32[]{:S(2)}) %all-to-all-start.6) | async-done | bytes 1572896 | tf_op jit(solution)/shard_map/all_to_all | solution.py:433
  171.1 1.2 copy-done.6
  172.3 9.5 %out_partial.1 = bf16[8,384,256]{2,1,0:T(8,128)(2,1)} custom-call(s32[8]{0:T(128)} %add_multiply_fusion.start_ref, bf16[384,2048]{1,0:T(8,128)(2,1)} %bitcast.33, bf16[256,2048]{1,0:T(8,128)(2,1)} %bitcast.6.refs_1_, bf16[256,2048]{1,0:T(8,128)(2,1)} %collective-permute-done.16.refs_2_, bf16[256,2048]{1,0:T(8,128)(2,1)} %copy-done.14, ...), custom_call_target="tpu_custom_call" | custom-call | flops 3221225472 | bytes 9961472 | tf_op jit(solution)/shard_map/out_partial/pallas_call | solution.py:309
  181.9 23.8 %all_to_all.41 = bf16[8,384,256]{2,1,0:T(8,128)(2,1)S(1)} all-to-all(bf16[8,384,256]{2,1,0:T(8,128)(2,1)} %out_partial.1), channel_id=1, replica_groups=mesh['zl'=2,'c'=2,'y'=4,'zh'=2,'x'=4] {'y','zh'}, dimensions={0} | all-to-all | bytes 3145728 | tf_op jit(solution)/shard_map/all_to_all | solution.py:443
  206.7 0.8 copy.25
  (86 shorter events, 4.5 us)
Async XLA Ops:
  3.3 15.3 %all-to-all-start = ((bf16[4,64,1280]{2,1,0:T(8,128)(2,1)}), bf16[4,64,1280]{2,1,0:T(8,128)(2,1)S(1)}, u32[]{:S(2)}, u32[]{:S(2)}) async-start(bf16[4,64,1280]{2,1,0:T(8,128)(2,1)} %joint_adam.2), calls=%async_computation | async-start | bytes 1310720 | tf_op jit(solution)/shard_map/all_to_all | solution.py:365
  7.7 3.3 %copy-start.15 = (bf16[8192]{0:T(1024)(128)(2,1)S(1)}, bf16[8192]{0:T(1024)(128)(2,1)}, u32[]{:S(2)}) copy-start(bf16[8192]{0:T(1024)(128)(2,1)} %param.14) | copy-start | bytes 49156
  7.7 3.4 %copy-start.13 = (bf16[4,6,8192]{2,0,1:T(4,128)(2,1)S(1)}, bf16[4,6,8192]{2,0,1:T(4,128)(2,1)}, u32[]{:S(2)}) copy-start(bf16[4,6,8192]{2,0,1:T(4,128)(2,1)} %param.13) | copy-start | bytes 1179652
  11.1 11.6 %copy-start.3 = (bf16[4,64,1280]{2,1,0:T(8,128)(2,1)S(1)}, bf16[4,64,1280]{2,1,0:T(8,128)(2,1)}, u32[]{:S(2)}) copy-start(bf16[4,64,1280]{2,1,0:T(8,128)(2,1)} %joint_adam.3) | copy-start | bytes 1966084
  18.6 18.0 %copy-start.5 = (bf16[4,64,1280]{2,1,0:T(8,128)(2,1)}, bf16[4,64,1280]{2,1,0:T(8,128)(2,1)S(1)}, u32[]{:S(2)}) copy-start(bf16[4,64,1280]{2,1,0:T(8,128)(2,1)S(1)} %all-to-all-done) | copy-start | bytes 1966084
  18.6 23.2 %collective-permute-start.2 = (bf16[256,1280]{1,0:T(8,128)(2,1)S(1)}, bf16[256,1280]{1,0:T(8,128)(2,1)}, u32[]{:S(2)}, u32[]{:S(2)}) collective-permute-start(bf16[256,1280]{1,0:T(8,128)(2,1)S(1)} %bitcast.29), channel_id=1, source_target_pairs={{0,32},{32,0},{1,33},{33,1},{2,34},{34,2},{3,35},{35,3},{4,36},{36... | collective-permute-start | bytes 1966088 | tf_op jit(solution)/shard_map/ppermute | solution.py:62
  18.6 23.2 %collective-permute-start.1 = (bf16[256,1280]{1,0:T(8,128)(2,1)S(1)}, bf16[256,1280]{1,0:T(8,128)(2,1)}, u32[]{:S(2)}, u32[]{:S(2)}) collective-permute-start(bf16[256,1280]{1,0:T(8,128)(2,1)S(1)} %bitcast.30), channel_id=1, source_target_pairs={{0,68},{64,0},{4,64},{68,4},{1,69},{65,1},{5,65},{69,5},{2,70},{66... | collective-permute-start | bytes 1966088 | tf_op jit(solution)/shard_map/ppermute | solution.py:56
  22.6 19.2 %collective-permute-start = (bf16[256,1280]{1,0:T(8,128)(2,1)S(1)}, bf16[256,1280]{1,0:T(8,128)(2,1)}, u32[]{:S(2)}, u32[]{:S(2)}) collective-permute-start(bf16[256,1280]{1,0:T(8,128)(2,1)S(1)} %bitcast.31), channel_id=1, source_target_pairs={{0,64},{64,4},{4,68},{68,0},{1,65},{65,5},{5,69},{69,1},{2,66},{66... | collective-permute-start | bytes 1966088 | tf_op jit(solution)/shard_map/ppermute | solution.py:56
  36.6 40.8 %copy-start.4 = (bf16[4,64,1280]{2,1,0:T(8,128)(2,1)}, bf16[4,64,1280]{2,1,0:T(8,128)(2,1)S(1)}, u32[]{:S(2)}) copy-start(bf16[4,64,1280]{2,1,0:T(8,128)(2,1)S(1)} %all_to_all.40) | copy-start | bytes 1966084
  36.6 28.8 %all-to-all-start.2 = ((bf16[16,24,2048]{2,1,0:T(8,128)(2,1)}), bf16[16,24,2048]{2,1,0:T(8,128)(2,1)S(1)}, u32[]{:S(2)}, u32[]{:S(2)}) async-start(bf16[16,24,2048]{2,1,0:T(8,128)(2,1)} %norm_rows.1), calls=%async_computation.2 | async-start | bytes 3145728 | tf_op jit(solution)/shard_map/all_to_all | solution.py:378
  41.8 7.8 %copy-start.16 = (s32[6]{0:T(128)S(1)}, s32[6]{0:T(128)}, u32[]{:S(2)}) copy-start(s32[6]{0:T(128)} %lengths_ref.3) | copy-start | bytes 76
  41.8 12.3 %collective-permute-start.6 = (bf16[256,1280]{1,0:T(8,128)(2,1)}, bf16[256,1280]{1,0:T(8,128)(2,1)}, u32[]{:S(2)}, u32[]{:S(2)}) collective-permute-start(bf16[256,1280]{1,0:T(8,128)(2,1)} %collective-permute-done.refs_5_), channel_id=1, source_target_pairs={{0,32},{32,0},{1,33},{33,1},{2,34},{34,2},{3,35},{35,3},{4,36},{36... | collective-permute-start | bytes 1966088 | tf_op jit(solution)/shard_map/ppermute | solution.py:62
  41.9 18.7 %collective-permute-start.3 = (bf16[256,1280]{1,0:T(8,128)(2,1)}, bf16[256,1280]{1,0:T(8,128)(2,1)}, u32[]{:S(2)}, u32[]{:S(2)}) collective-permute-start(bf16[256,1280]{1,0:T(8,128)(2,1)} %collective-permute-done.refs_5_), channel_id=1, source_target_pairs={{0,64},{64,4},{4,68},{68,0},{1,65},{65,5},{5,69},{69,1},{2,66},{66... | collective-permute-start | bytes 1966088 | tf_op jit(solution)/shard_map/ppermute | solution.py:56
  42.0 18.6 %collective-permute-start.7 = (bf16[256,1280]{1,0:T(8,128)(2,1)S(1)}, bf16[256,1280]{1,0:T(8,128)(2,1)}, u32[]{:S(2)}, u32[]{:S(2)}) collective-permute-start(bf16[256,1280]{1,0:T(8,128)(2,1)S(1)} %bitcast.25), channel_id=1, source_target_pairs={{0,32},{32,0},{1,33},{33,1},{2,34},{34,2},{3,35},{35,3},{4,36},{36... | collective-permute-start | bytes 1966088 | tf_op jit(solution)/shard_map/ppermute | solution.py:62
  42.4 18.2 %collective-permute-start.4 = (bf16[256,1280]{1,0:T(8,128)(2,1)S(1)}, bf16[256,1280]{1,0:T(8,128)(2,1)}, u32[]{:S(2)}, u32[]{:S(2)}) collective-permute-start(bf16[256,1280]{1,0:T(8,128)(2,1)S(1)} %bitcast.26), channel_id=1, source_target_pairs={{0,68},{64,0},{4,64},{68,4},{1,69},{65,1},{5,65},{69,5},{2,70},{66... | collective-permute-start | bytes 1966088 | tf_op jit(solution)/shard_map/ppermute | solution.py:56
  45.4 8.7 %collective-permute-start.5 = (bf16[256,1280]{1,0:T(8,128)(2,1)}, bf16[256,1280]{1,0:T(8,128)(2,1)}, u32[]{:S(2)}, u32[]{:S(2)}) collective-permute-start(bf16[256,1280]{1,0:T(8,128)(2,1)} %collective-permute-done.1.refs_3_), channel_id=1, source_target_pairs={{0,32},{32,0},{1,33},{33,1},{2,34},{34,2},{3,35},{35,3},{4,36},{36... | collective-permute-start | bytes 1966088 | tf_op jit(solution)/shard_map/ppermute | solution.py:62
  60.6 9.1 %collective-permute-start.8 = (bf16[256,1280]{1,0:T(8,128)(2,1)}, bf16[256,1280]{1,0:T(8,128)(2,1)S(1)}, u32[]{:S(2)}, u32[]{:S(2)}) collective-permute-start(bf16[256,1280]{1,0:T(8,128)(2,1)} %collective-permute-done.3.refs_7_), channel_id=1, source_target_pairs={{0,32},{32,0},{1,33},{33,1},{2,34},{34,2},{3,35},{35,3},{4,36},{36... | collective-permute-start | bytes 1966088 | tf_op jit(solution)/shard_map/ppermute | solution.py:62
  65.4 4.3 %copy-start = (bf16[16,24,2048]{2,1,0:T(8,128)(2,1)}, bf16[16,24,2048]{2,1,0:T(8,128)(2,1)S(1)}, u32[]{:S(2)}) copy-start(bf16[16,24,2048]{2,1,0:T(8,128)(2,1)S(1)} %all-to-all-done.2) | copy-start | bytes 4718596
  65.4 17.2 %all-to-all-start.4 = ((bf16[4,64,2048]{2,1,0:T(8,128)(2,1)}), bf16[4,64,2048]{2,1,0:T(8,128)(2,1)}, u32[]{:S(2)}, u32[]{:S(2)}) async-start(bf16[4,64,2048]{2,1,0:T(8,128)(2,1)} %reshape.87), calls=%async_computation.4 | async-start | bytes 2097152 | tf_op jit(solution)/shard_map/all_to_all | solution.py:365
  77.4 15.3 %collective-permute-start.10 = (bf16[256,1280]{1,0:T(8,128)(2,1)S(1)}, bf16[256,1280]{1,0:T(8,128)(2,1)S(1)}, u32[]{:S(2)}, u32[]{:S(2)}) collective-permute-start(bf16[256,1280]{1,0:T(8,128)(2,1)S(1)} %bitcast.27), channel_id=1, source_target_pairs={{0,64},{64,4},{4,68},{68,0},{1,65},{65,5},{5,69},{69,1},{2,66},{66... | collective-permute-start | bytes 1966088 | tf_op jit(solution)/shard_map/ppermute | solution.py:56
  77.4 15.3 %collective-permute-start.12 = (bf16[256,1280]{1,0:T(8,128)(2,1)}, bf16[256,1280]{1,0:T(8,128)(2,1)S(1)}, u32[]{:S(2)}, u32[]{:S(2)}) collective-permute-start(bf16[256,1280]{1,0:T(8,128)(2,1)} %collective-permute-done.4.refs_3_), channel_id=1, source_target_pairs={{0,68},{64,0},{4,64},{68,4},{1,69},{65,1},{5,65},{69,5},{2,70},{66... | collective-permute-start | bytes 1966088 | tf_op jit(solution)/shard_map/ppermute | solution.py:56
  82.6 20.9 %all-to-all-start.3 = ((bf16[16,24,1280]{2,1,0:T(8,128)(2,1)}), bf16[16,24,1280]{2,1,0:T(8,128)(2,1)S(1)}, u32[]{:S(2)}, u32[]{:S(2)}) async-start(bf16[16,24,1280]{2,1,0:T(8,128)(2,1)} %bitcast.22), calls=%async_computation.3 | async-start | bytes 1966080 | tf_op jit(solution)/shard_map/all_to_all | solution.py:409
  87.8 5.4 %collective-permute-start.9 = (bf16[256,1280]{1,0:T(8,128)(2,1)}, bf16[256,1280]{1,0:T(8,128)(2,1)S(1)}, u32[]{:S(2)}, u32[]{:S(2)}) collective-permute-start(bf16[256,1280]{1,0:T(8,128)(2,1)} %collective-permute-done.4.refs_3_), channel_id=1, source_target_pairs={{0,32},{32,0},{1,33},{33,1},{2,34},{34,2},{3,35},{35,3},{4,36},{36... | collective-permute-start | bytes 1966088 | tf_op jit(solution)/shard_map/ppermute | solution.py:62
  92.7 3.0 %copy-start.7 = (bf16[256,1280]{1,0:T(8,128)(2,1)}, bf16[256,1280]{1,0:T(8,128)(2,1)S(1)}, u32[]{:S(2)}) copy-start(bf16[256,1280]{1,0:T(8,128)(2,1)S(1)} %collective-permute-done.10.refs_5_) | copy-start | bytes 1966084
  92.7 2.1 %collective-permute-start.11 = (bf16[256,1280]{1,0:T(8,128)(2,1)S(1)}, bf16[256,1280]{1,0:T(8,128)(2,1)S(1)}, u32[]{:S(2)}, u32[]{:S(2)}) collective-permute-start(bf16[256,1280]{1,0:T(8,128)(2,1)S(1)} %collective-permute-done.10.refs_5_), channel_id=1, source_target_pairs={{0,32},{32,0},{1,33},{33,1},{2,34},{34,2},{3,35},{35,3},{4,36},{36... | collective-permute-start | bytes 1966088 | tf_op jit(solution)/shard_map/ppermute | solution.py:62
  92.7 3.0 %copy-start.8 = (bf16[256,1280]{1,0:T(8,128)(2,1)}, bf16[256,1280]{1,0:T(8,128)(2,1)S(1)}, u32[]{:S(2)}) copy-start(bf16[256,1280]{1,0:T(8,128)(2,1)S(1)} %collective-permute-done.12.refs_7_) | copy-start | bytes 1966084
  92.7 3.0 %collective-permute-start.13 = (bf16[256,1280]{1,0:T(8,128)(2,1)S(1)}, bf16[256,1280]{1,0:T(8,128)(2,1)S(1)}, u32[]{:S(2)}, u32[]{:S(2)}) collective-permute-start(bf16[256,1280]{1,0:T(8,128)(2,1)S(1)} %collective-permute-done.12.refs_7_), channel_id=1, source_target_pairs={{0,32},{32,0},{1,33},{33,1},{2,34},{34,2},{3,35},{35,3},{4,36},{36... | collective-permute-start | bytes 1966088 | tf_op jit(solution)/shard_map/ppermute | solution.py:62
  93.2 2.5 %copy-start.10 = (bf16[256,1280]{1,0:T(8,128)(2,1)}, bf16[256,1280]{1,0:T(8,128)(2,1)S(1)}, u32[]{:S(2)}) copy-start(bf16[256,1280]{1,0:T(8,128)(2,1)S(1)} %collective-permute-done.9.refs_4_) | copy-start | bytes 1966084
  94.8 0.9 copy-start.11
  95.7 0.9 copy-start.12
  103.5 9.8 %copy-start.1 = (bf16[16,24,1280]{2,1,0:T(8,128)(2,1)}, bf16[16,24,1280]{2,1,0:T(8,128)(2,1)S(1)}, u32[]{:S(2)}) copy-start(bf16[16,24,1280]{2,1,0:T(8,128)(2,1)S(1)} %all-to-all-done.3) | copy-start | bytes 2949124
  103.5 26.8 %collective-permute-start.16 = (bf16[256,2048]{1,0:T(8,128)(2,1)}, bf16[256,2048]{1,0:T(8,128)(2,1)}, u32[]{:S(2)}, u32[]{:S(2)}) collective-permute-start(bf16[256,2048]{1,0:T(8,128)(2,1)} %bitcast.6.refs_1_), channel_id=1, source_target_pairs={{0,32},{32,0},{1,33},{33,1},{2,34},{34,2},{3,35},{35,3},{4,36},{36... | collective-permute-start | bytes 3145736 | tf_op jit(solution)/shard_map/ppermute | solution.py:62
  103.7 27.1 %collective-permute-start.15 = (bf16[256,2048]{1,0:T(8,128)(2,1)}, bf16[256,2048]{1,0:T(8,128)(2,1)S(1)}, u32[]{:S(2)}, u32[]{:S(2)}) collective-permute-start(bf16[256,2048]{1,0:T(8,128)(2,1)} %bitcast.6.refs_1_), channel_id=1, source_target_pairs={{0,68},{64,0},{4,64},{68,4},{1,69},{65,1},{5,65},{69,5},{2,70},{66... | collective-permute-start | bytes 3145736 | tf_op jit(solution)/shard_map/ppermute | solution.py:56
  107.4 26.8 %collective-permute-start.14 = (bf16[256,2048]{1,0:T(8,128)(2,1)}, bf16[256,2048]{1,0:T(8,128)(2,1)}, u32[]{:S(2)}, u32[]{:S(2)}) collective-permute-start(bf16[256,2048]{1,0:T(8,128)(2,1)} %bitcast.6.refs_1_), channel_id=1, source_target_pairs={{0,64},{64,4},{4,68},{68,0},{1,65},{65,5},{5,69},{69,1},{2,66},{66... | collective-permute-start | bytes 3145736 | tf_op jit(solution)/shard_map/ppermute | solution.py:56
  107.4 22.9 %all-to-all-start.5 = ((bf16[16,24,1280]{2,1,0:T(8,128)(2,1)}), bf16[16,24,1280]{2,1,0:T(8,128)(2,1)S(1)}, u32[]{:S(2)}, u32[]{:S(2)}) async-start(bf16[16,24,1280]{2,1,0:T(8,128)(2,1)} %bitcast.23), calls=%async_computation.5 | async-start | bytes 1966080 | tf_op jit(solution)/shard_map/all_to_all | solution.py:421
  130.3 3.9 %copy-start.2 = (bf16[16,24,1280]{2,1,0:T(8,128)(2,1)}, bf16[16,24,1280]{2,1,0:T(8,128)(2,1)S(1)}, u32[]{:S(2)}) copy-start(bf16[16,24,1280]{2,1,0:T(8,128)(2,1)S(1)} %all-to-all-done.5) | copy-start | bytes 2949124
  130.8 21.5 %copy-start.14 = (bf16[256,2048]{1,0:T(8,128)(2,1)}, bf16[256,2048]{1,0:T(8,128)(2,1)S(1)}, u32[]{:S(2)}) copy-start(bf16[256,2048]{1,0:T(8,128)(2,1)S(1)} %collective-permute-done.15.refs_3_) | copy-start | bytes 3145732
  142.0 29.1 %all-to-all-start.6 = ((bf16[16,3,8,2048]{3,2,1,0:T(8,128)(2,1)}), bf16[16,3,8,2048]{3,2,1,0:T(8,128)(2,1)S(1)}, u32[]{:S(2)}, u32[]{:S(2)}) async-start(bf16[16,3,8,2048]{3,2,1,0:T(8,128)(2,1)} %attention.3), calls=%async_computation.6 | async-start | bytes 3145728 | tf_op jit(solution)/shard_map/all_to_all | solution.py:433
  148.8 14.1 %collective-permute-start.19 = (bf16[128,2048]{1,0:T(8,128)(2,1)S(1)}, bf16[128,2048]{1,0:T(8,128)(2,1)S(1)}, u32[]{:S(2)}, u32[]{:S(2)}) collective-permute-start(bf16[128,2048]{1,0:T(8,128)(2,1)S(1)} %slice.6), channel_id=1, source_target_pairs={{0,64},{64,4},{4,68},{68,0},{1,65},{65,5},{5,69},{69,1},{2,66},{66... | collective-permute-start | bytes 1572872 | tf_op jit(solution)/shard_map/ppermute | solution.py:56
  149.0 13.9 %collective-permute-start.21 = (bf16[128,2048]{1,0:T(8,128)(2,1)S(1)}, bf16[128,2048]{1,0:T(8,128)(2,1)S(1)}, u32[]{:S(2)}, u32[]{:S(2)}) collective-permute-start(bf16[128,2048]{1,0:T(8,128)(2,1)S(1)} %slice.7), channel_id=1, source_target_pairs={{0,68},{64,0},{4,64},{68,4},{1,69},{65,1},{5,65},{69,5},{2,70},{66... | collective-permute-start | bytes 1572872 | tf_op jit(solution)/shard_map/ppermute | solution.py:56
  152.3 13.3 %collective-permute-start.17 = (bf16[256,2048]{1,0:T(8,128)(2,1)S(1)}, bf16[256,2048]{1,0:T(8,128)(2,1)S(1)}, u32[]{:S(2)}, u32[]{:S(2)}) collective-permute-start(bf16[256,2048]{1,0:T(8,128)(2,1)S(1)} %collective-permute-done.15.refs_3_), channel_id=1, source_target_pairs={{0,32},{32,0},{1,33},{33,1},{2,34},{34,2},{3,35},{35,3},{4,36},{36... | collective-permute-start | bytes 3145736 | tf_op jit(solution)/shard_map/ppermute | solution.py:62
  152.3 15.1 %collective-permute-start.18 = (bf16[256,2048]{1,0:T(8,128)(2,1)}, bf16[256,2048]{1,0:T(8,128)(2,1)}, u32[]{:S(2)}, u32[]{:S(2)}) collective-permute-start(bf16[256,2048]{1,0:T(8,128)(2,1)} %collective-permute-done.14.refs_5_), channel_id=1, source_target_pairs={{0,32},{32,0},{1,33},{33,1},{2,34},{34,2},{3,35},{35,3},{4,36},{36... | collective-permute-start | bytes 3145736 | tf_op jit(solution)/shard_map/ppermute | solution.py:62
  162.9 8.2 %copy-start.18 = (bf16[128,2048]{1,0:T(8,128)(2,1)}, bf16[128,2048]{1,0:T(8,128)(2,1)S(1)}, u32[]{:S(2)}) copy-start(bf16[128,2048]{1,0:T(8,128)(2,1)S(1)} %collective-permute-done.19.refs_7_) | copy-start | bytes 1572868
  162.9 1.9 collective-permute-start.20
  162.9 2.7 %copy-start.19 = (bf16[128,2048]{1,0:T(8,128)(2,1)}, bf16[128,2048]{1,0:T(8,128)(2,1)S(1)}, u32[]{:S(2)}) copy-start(bf16[128,2048]{1,0:T(8,128)(2,1)S(1)} %collective-permute-done.21.refs_9_) | copy-start | bytes 1572868
  162.9 2.6 %collective-permute-start.22 = (bf16[128,2048]{1,0:T(8,128)(2,1)S(1)}, bf16[128,2048]{1,0:T(8,128)(2,1)S(1)}, u32[]{:S(2)}, u32[]{:S(2)}) collective-permute-start(bf16[128,2048]{1,0:T(8,128)(2,1)S(1)} %collective-permute-done.21.refs_9_), channel_id=1, source_target_pairs={{0,32},{32,0},{1,33},{33,1},{2,34},{34,2},{3,35},{35,3},{4,36},{36... | collective-permute-start | bytes 1572872 | tf_op jit(solution)/shard_map/ppermute | solution.py:62
  166.4 1.0 copy-start.17
  171.1 1.2 copy-start.6
  (3 other events, 2.5 us)
